TPU v7x, 128 devices: a whole 4x4x4 slice. The times are simulated.
128 devices in a mesh: slab: 4 (over x_lo, core), brick: 32 (over z, y, x_hi).
Axes of the slice: x: 4 (x_hi: 2, x_lo: 2; x = x_hi * 2 + x_lo), y: 4, z: 4, core: 2. Of those that a mesh axis runs over, the one named last changes fastest.
Arguments:
- positions: float32 [3, 4, 32, 128], P(None, 'slab', 'brick'), may hold values from 0 to 56, as said below
- species: int32 [4, 32, 128], P('slab', 'brick'), may hold values from 0 to 4
- export_index: int32 [4, 32, 128], P('slab', 'brick'), may hold values from 0 to 127
- edge_center: int32 [4, 32, 256], P('slab', 'brick'), may hold values from 0 to 127
- edge_neighbor: int32 [4, 32, 256], P('slab', 'brick'), may hold values from 0 to 1279
- edge_count: int32 [4, 32], P('slab', 'brick'), may hold values from 64 to 256, as said below
- force_target: float32 [3, 4, 32, 128], P(None, 'slab', 'brick'), may hold values from -6 to 6
- radial_weight: float32 [8, 512], replicated, may hold values from -2 to 2
- center_embed: float32 [5, 512], replicated, may hold values from -6 to 6
- neighbor_embed: float32 [5, 512], replicated, may hold values from -6 to 6
- environment_weight: float32 [2, 512, 64], replicated, may hold values from -0.25 to 0.25
- latent_weight: float32 [2, 576, 512], replicated, may hold values from -0.25 to 0.25
- output_weight: float32 [512], replicated, may hold values from -0.25 to 0.25
Outputs:
- forces: float32 [3, 4, 32, 128], P(None, 'slab', 'brick')
- grad_radial: float32 [8, 512], replicated
- grad_center: float32 [5, 512], replicated
- grad_neighbor: float32 [5, 512], replicated
- grad_environment: float32 [2, 512, 64], replicated
- grad_latent: float32 [2, 576, 512], replicated
- grad_output: float32 [512], replicated
Inputs may be any that keep to these rules, and one draw needn't show every extreme that they name: `positions`: atom of domain (s, b) has first coordinate in [0, 1.75), second in [1.75 b, 1.75 (b + 1)), third in [1.75 s, 1.75 (s + 1)). `edge_count`: one domain has all 256 slots live in every draw.
All inputs are finite; a program needn't handle non-finite values.
Results may differ from a plain program's by a relative error of at most 0.0003.
Values sent between devices are 32-bit elements; how exact they have to be, the bound alone decides.
A program may use at most 64 MiB of HBM per device.

v0:
```python
import math

import jax
import jax.numpy as jnp
from jax import lax
from jax.sharding import PartitionSpec as P

cell_width = 1.75
cutoff_radius = 6.0
softening = 0.25


def with_halo(x, sides, width):
    for axis, dim in sides:
        devices, length = (lax.axis_size(axis), x.shape[dim])
        up = [(i, (i + 1) % devices) for i in range(devices)]
        down = [(j, i) for i, j in up]
        last = lax.slice_in_dim(x, length - width, length, axis=dim)
        initial = lax.slice_in_dim(x, 0, width, axis=dim)
        before = lax.ppermute(last, axis, up)
        after = lax.ppermute(initial, axis, down)
        x = jnp.concatenate([before, x, after], axis=dim)
    return x


def passed_along(x, axis, by):
    devices = lax.axis_size(axis)
    return lax.ppermute(x, axis, [(i, (i + by) % devices) for i in range(devices)])


def product(left, right):
    return jnp.dot(left, right, precision=lax.Precision.HIGHEST, preferred_element_type=jnp.float32)


def species_onehot(values, count):
    return (values[None, :] == jnp.arange(count, dtype=jnp.int32)[:, None]).astype(jnp.float32)


def edge_energy(params, table_pos, table_hot, center, neighbor, live, atom_count):
    (
        radial_weight,
        center_embed,
        neighbor_embed,
        environment_weight,
        latent_weight,
        output_weight,
    ) = params
    hidden_width = radial_weight.shape[1]
    multiplicity = environment_weight.shape[2]
    edge_slots = center.shape[0]
    vectors = table_pos[:, neighbor] - table_pos[:, center]
    squared = jnp.sum(vectors * vectors, axis=0) + softening
    distance = jnp.sqrt(squared)
    envelope = (1.0 - squared / (cutoff_radius * cutoff_radius)) ** 2 * live
    directions = vectors / distance[None, :]
    orders = jnp.arange(1, radial_weight.shape[0] + 1, dtype=jnp.float32)
    basis = (
        jnp.sin(orders[:, None] * (math.pi / cutoff_radius) * distance[None, :]) / distance[None, :]
    )
    atom_hot = (center[None, :] == jnp.arange(atom_count, dtype=jnp.int32)[:, None]).astype(
        jnp.float32
    )
    latent = jax.nn.silu(
        product(radial_weight.T, basis)
        + product(center_embed.T, table_hot[:, center])
        + product(neighbor_embed.T, table_hot[:, neighbor])
    )
    for layer_index in range(environment_weight.shape[0]):
        weights = product(environment_weight[layer_index].T, latent) * envelope[None, :]
        tensors = (directions[:, None, :] * weights[None, :, :]).reshape(
            3 * multiplicity, edge_slots
        )
        summed = product(tensors, atom_hot.T)
        spread = product(summed, atom_hot)
        invariant = jnp.sum((tensors * spread).reshape(3, multiplicity, edge_slots), axis=0)
        update = product(latent_weight[layer_index][:hidden_width].T, latent) + product(
            latent_weight[layer_index][hidden_width:].T, invariant
        )
        latent = latent + jax.nn.silu(update)
    return jnp.sum(product(output_weight[None, :], latent)[0] * envelope)


def image_offsets():
    slab_index = lax.axis_index("slab")
    brick_index = lax.axis_index("brick")
    slab_total = lax.axis_size("slab")
    brick_total = lax.axis_size("brick")
    steps = jnp.arange(3, dtype=jnp.int32) - 1
    cross_z = ((slab_index + steps + slab_total) // slab_total - 1).astype(jnp.float32) * (
        slab_total * cell_width
    )
    cross_y = ((brick_index + steps + brick_total) // brick_total - 1).astype(jnp.float32) * (
        brick_total * cell_width
    )
    zeros_plane = jnp.zeros((3, 3), jnp.float32)
    offsets = jnp.stack(
        [
            zeros_plane,
            jnp.broadcast_to(cross_y[None, :], (3, 3)),
            jnp.broadcast_to(cross_z[:, None], (3, 3)),
        ],
        axis=2,
    )
    return offsets[..., None]


def on_device(
    positions,
    species,
    export_index,
    edge_center,
    edge_neighbor,
    edge_count,
    force_target,
    radial_weight,
    center_embed,
    neighbor_embed,
    environment_weight,
    latent_weight,
    output_weight,
):
    params = (
        radial_weight,
        center_embed,
        neighbor_embed,
        environment_weight,
        latent_weight,
        output_weight,
    )
    own_pos = positions[:, 0, 0]
    atom_count = own_pos.shape[1]
    exports = export_index[0, 0]
    ghost_count = exports.shape[0]
    species_count = center_embed.shape[0]
    own_species = species[0, 0]
    center = edge_center[0, 0]
    neighbor = edge_neighbor[0, 0]
    live = (jnp.arange(center.shape[0], dtype=jnp.int32) < edge_count[0, 0]).astype(jnp.float32)
    outgoing = jnp.concatenate(
        [own_pos[:, exports], own_species[exports].astype(jnp.float32)[None]], axis=0
    )
    beside_all = with_halo(outgoing[None, None], (("slab", 0), ("brick", 1)), 1)
    ghost_pos = beside_all[:, :, :3] + image_offsets()
    ghost_table = jnp.transpose(ghost_pos, (2, 0, 1, 3)).reshape(3, 9 * ghost_count)
    ghost_ids = beside_all[:, :, 3].reshape(9 * ghost_count).astype(jnp.int32)
    table_pos = jnp.concatenate([own_pos, ghost_table], axis=1)
    table_hot = jnp.concatenate(
        [species_onehot(own_species, species_count), species_onehot(ghost_ids, species_count)],
        axis=1,
    )
    gradient = jax.grad(edge_energy, argnums=1)(
        params, table_pos, table_hot, center, neighbor, live, atom_count
    )
    own_grad = gradient[:, :atom_count]
    ghost_grad = jnp.transpose(gradient[:, atom_count:].reshape(3, 3, 3, ghost_count), (1, 2, 0, 3))
    returned = ghost_grad[1, 1]
    for row in range(3):
        for column in range(3):
            if row != 1 or column != 1:
                piece = ghost_grad[row, column]
                if column != 1:
                    piece = passed_along(piece, "brick", column - 1)
                if row != 1:
                    piece = passed_along(piece, "slab", row - 1)
                returned = returned + piece
    total_grad = own_grad.at[:, exports].add(returned)
    forces = -total_grad
    cotangent = 2.0 * (forces - force_target[:, 0, 0]) / (3.0 * atom_count)
    tangent_around = with_halo(cotangent[:, exports][None, None], (("slab", 0), ("brick", 1)), 1)
    tangent_table = jnp.concatenate(
        [cotangent, jnp.transpose(tangent_around, (2, 0, 1, 3)).reshape(3, 9 * ghost_count)], axis=1
    )

    def param_gradient(position_table):
        return jax.grad(edge_energy, argnums=0)(
            params, position_table, table_hot, center, neighbor, live, atom_count
        )

    unused, tangents = jax.jvp(param_gradient, (table_pos,), (tangent_table,))
    local = tuple((-value for value in tangents))
    grads = lax.psum(local, ("slab", "brick"))
    return (forces[:, None, None, :], grads[0], grads[1], grads[2], grads[3], grads[4], grads[5])


def solution(mesh):
    return jax.shard_map(
        on_device,
        mesh=mesh,
        in_specs=(
            P(None, "slab", "brick", None),
            P("slab", "brick", None),
            P("slab", "brick", None),
            P("slab", "brick", None),
            P("slab", "brick", None),
            P("slab", "brick"),
            P(None, "slab", "brick", None),
            P(),
            P(),
            P(),
            P(),
            P(),
            P(),
        ),
        out_specs=(P(None, "slab", "brick", None), P(), P(), P(), P(), P(), P()),
        check_vma=False,
    )
```

profile of v0, /device:TPU:1, one launch (start us, length us, event | category | flops | bytes accessed | tf_op | source)
XLA Modules:
  0.0 331.8 jit_solution(12855858141429852250)
XLA Ops:
  7.9 1.6 gather_fusion.1
  11.1 1.5 collective-permute-start.1
  12.5 1.3 collective-permute-start
  16.1 8.6 %collective-permute-start.3 = (f32[3,1,4,128]{3,2,1,0:T(4,128)S(1)}, f32[3,1,4,128]{3,2,1,0:T(4,128)S(1)}, u32[]{:S(2)}, u32[]{:S(2)}) collective-permute-start(f32[3,1,4,128]{3,2,1,0:T(4,128)S(1)} %pad_maximum_fusion.4), channel_id=1, source_target_pairs={{1,0},{2,1},{3,2},{4,3},{5,4},{6,5},{7,6},{8,7},{9,8},{10,9},{11,1... | collective-permute-start | bytes 18440 | tf_op jit(solution)/shard_map/ppermute | solution.py:21
  25.6 7.5 %collective-permute-done.2 = f32[3,1,4,128]{3,2,1,0:T(4,128)S(1)} collective-permute-done((f32[3,1,4,128]{3,2,1,0:T(4,128)S(1)}, f32[3,1,4,128]{3,2,1,0:T(4,128)S(1)}, u32[]{:S(2)}, u32[]{:S(2)}) %collective-permute-start.2) | collective-permute-done | bytes 6176 | tf_op jit(solution)/shard_map/ppermute | solution.py:20
  41.2 2.3 fusion.36
  43.5 1.5 multiply_add_fusion.4
  45.1 1.2 broadcast_multiply_fusion.4
  47.2 0.9 bitcast_multiply_fusion.33
  48.7 1.5 fusion.109
  50.2 2.1 fusion.3
  53.2 1.2 fusion.16
  56.4 1.3 fusion.14
  57.8 0.8 fusion.87
  60.9 3.2 scatter_custom_fusion
  64.1 1.1 slice.130
  65.3 0.8 copy-done.16
  66.2 3.0 collective-permute-start.14
  69.2 2.1 collective-permute-start.13
  71.3 4.6 %collective-permute-start.11 = (f32[3,128]{0,1:T(8,128)S(1)}, f32[3,128]{0,1:T(8,128)}, u32[]{:S(2)}, u32[]{:S(2)}) collective-permute-start(f32[3,128]{0,1:T(8,128)S(1)} %get-tuple-element.117), channel_id=1, source_target_pairs={{0,31},{1,0},{2,1},{3,2},{4,3},{5,4},{6,5},{7,6},{8,7},{9,8},{10,9... | collective-permute-start | bytes 4616 | tf_op jit(solution)/shard_map/ppermute | solution.py:28
  75.9 7.2 %collective-permute-start.9 = (f32[3,128]{0,1:T(8,128)S(1)}, f32[3,128]{0,1:T(8,128)S(1)}, u32[]{:S(2)}, u32[]{:S(2)}) collective-permute-start(f32[3,128]{0,1:T(8,128)S(1)} %get-tuple-element.119), channel_id=1, source_target_pairs={{0,31},{1,0},{2,1},{3,2},{4,3},{5,4},{6,5},{7,6},{8,7},{9,8},{10,9... | collective-permute-start | bytes 4616 | tf_op jit(solution)/shard_map/ppermute | solution.py:28
  83.9 1.5 collective-permute-done.10
  86.3 5.7 %collective-permute-done.7 = f32[3,128]{0,1:T(8,128)} collective-permute-done((f32[3,128]{0,1:T(8,128)S(1)}, f32[3,128]{0,1:T(8,128)}, u32[]{:S(2)}, u32[]{:S(2)}) %collective-permute-start.7) | collective-permute-done | bytes 1568 | tf_op jit(solution)/shard_map/ppermute | solution.py:28
  92.0 1.6 collective-permute-start.8
  93.8 2.2 collective-permute-done.8
  95.9 1.6 scatter_custom_fusion.1
  98.4 1.7 collective-permute-start.16
  100.2 1.9 collective-permute-done.17
  102.1 2.8 collective-permute-start.19
  106.3 2.0 collective-permute-done.19
  108.3 1.0 copy.86
  109.4 6.9 %collective-permute-done.18 = f32[3,1,3,128]{2,3,1,0:T(8,128)S(1)} collective-permute-done((f32[3,1,3,128]{2,3,1,0:T(8,128)S(1)}, f32[3,1,3,128]{2,3,1,0:T(8,128)S(1)}, u32[]{:S(2)}, u32[]{:S(2)}) %collective-permute-start.18) | collective-permute-done | bytes 4640 | tf_op jit(solution)/shard_map/ppermute | solution.py:20
  116.4 1.1 copy.87
  117.5 2.0 pad_maximum_fusion.1
  119.5 2.0 gather_fusion.6
  121.5 1.9 gather_fusion.5
  123.7 2.7 fusion.81
  127.8 0.9 multiply_add_fusion.7
  130.0 1.1 fusion.1
  131.1 1.7 fusion.80
  135.7 1.1 multiply_add_fusion.5
  136.8 1.6 reduce_sum.211
  138.3 1.6 reduce_sum.210
  139.9 1.5 fusion.106
  141.4 1.5 fusion.104
  142.9 1.1 fusion
  144.0 1.4 fusion.60
  146.5 1.0 fusion.276
  147.5 1.0 convolution_bitcast_fusion.16
  148.5 1.2 fusion.9
  149.7 1.1 fusion.11
  153.1 1.0 fusion.56
  155.2 1.1 fusion.5
  156.9 1.1 fusion.264
  160.2 1.3 convolution_add_fusion.1
  161.5 1.3 fusion.7
  166.1 1.0 convolution_add_fusion
  168.3 2.0 add_negate_fusion
  170.3 0.9 copy-done.7
  171.6 1.0 fusion.52
  174.2 65.0 %all-reduce.10 = (f32[8,512]{1,0:T(8,128)}, f32[5,512]{1,0:T(8,128)}, f32[5,512]{1,0:T(8,128)}, f32[512]{0:T(512)}) all-reduce(f32[8,512]{1,0:T(8,128)S(1)} %fusion.25, f32[5,512]{1,0:T(8,128)S(1)} %convolution_negate_fusion.1, f32[5,512]{1,0:T(8,128)S(1)} %convolution_negate_fusion, ...), channel_id=1, replica_groups=mesh['slab'=4,'brick'=32] {'slab','brick'}, use_global_device_ids=true, to_apply=%region_23.26 | all-reduce | flops 9728 | bytes 77824 | tf_op jit(solution)/shard_map/psum | solution.py:181
  239.1 80.7 %all-reduce.14.cloned.1.call-done = (f32[2,512,64]{1,2,0:T(8,128)}, f32[2,576,512]{2,1,0:T(8,128)}) async-done(((f32[2,512,64]{1,2,0:T(8,128)}, f32[2,576,512]{2,1,0:T(8,128)}), (f32[2,512,64]{1,2,0:T(8,128)}, f32[2,576,512]{2,1,0:T(8,128)})) %all-reduce.14.cloned.1.call-update) | async-done | bytes 2621456 | tf_op jit(solution)/shard_map/psum | solution.py:181
  319.8 1.7 copy.99
  321.5 3.3 copy.100
  (329 shorter events, 42.4 us)
Async XLA Ops:
  7.2 30.6 %copy-start = (f32[8,512]{1,0:T(8,128)S(1)}, f32[8,512]{1,0:T(8,128)}, u32[]{:S(2)}) copy-start(f32[8,512]{1,0:T(8,128)} %param.30) | copy-start | bytes 49156
  7.2 31.4 %copy-start.63 = (f32[5,512]{1,0:T(8,128)S(1)}, f32[5,512]{1,0:T(8,128)}, u32[]{:S(2)}) copy-start(f32[5,512]{1,0:T(8,128)} %param.31) | copy-start | bytes 30724
  7.2 312.6 %all-reduce.14.cloned.1.call-start = ((), (), s32[]{:S(2)}) async-start(), calls=%async_computation | async-start | bytes 5242880 | tf_op jit(solution)/shard_map/psum | solution.py:181
  7.9 2.4 copy-start.78
  7.9 3.1 copy-start.71
  9.5 29.4 %copy-start.64 = (f32[5,512]{1,0:T(8,128)S(1)}, f32[5,512]{1,0:T(8,128)}, u32[]{:S(2)}) copy-start(f32[5,512]{1,0:T(8,128)} %param.32) | copy-start | bytes 30724
  11.1 5.0 %collective-permute-start.1 = (f32[1,1,4,128]{3,2,1,0:T(4,128)S(1)}, f32[1,1,4,128]{3,2,1,0:T(4,128)S(1)}, u32[]{:S(2)}, u32[]{:S(2)}) collective-permute-start(f32[1,1,4,128]{3,2,1,0:T(4,128)S(1)} %maximum_bitcast_fusion.2), channel_id=1, source_target_pairs={{32,0},{64,32},{96,64},{0,96},{33,1},{65,33},{97,65},{1,97},{34,2}... | collective-permute-start | bytes 6152 | tf_op jit(solution)/shard_map/ppermute | solution.py:21
  12.5 3.5 %collective-permute-start = (f32[1,1,4,128]{3,2,1,0:T(4,128)S(1)}, f32[1,1,4,128]{3,2,1,0:T(4,128)S(1)}, u32[]{:S(2)}, u32[]{:S(2)}) collective-permute-start(f32[1,1,4,128]{3,2,1,0:T(4,128)S(1)} %maximum_bitcast_fusion.2), channel_id=1, source_target_pairs={{0,32},{32,64},{64,96},{96,0},{1,33},{33,65},{65,97},{97,1},{2,34}... | collective-permute-start | bytes 6152 | tf_op jit(solution)/shard_map/ppermute | solution.py:20
  15.2 21.9 %copy-start.67 = (s32[1024]{0:T(1024)}, s32[1024]{0:T(1024)S(1)}, u32[]{:S(2)}) copy-start(s32[1024]{0:T(1024)S(1)} %pad_clamp_fusion) | copy-start | bytes 12292
  15.2 21.0 %copy-start.68 = (s32[1024]{0:T(1024)}, s32[1024]{0:T(1024)S(1)}, u32[]{:S(2)}) copy-start(s32[1024]{0:T(1024)S(1)} %pad_clamp_fusion.1) | copy-start | bytes 12292
  16.1 9.5 %collective-permute-start.3 = (f32[3,1,4,128]{3,2,1,0:T(4,128)S(1)}, f32[3,1,4,128]{3,2,1,0:T(4,128)S(1)}, u32[]{:S(2)}, u32[]{:S(2)}) collective-permute-start(f32[3,1,4,128]{3,2,1,0:T(4,128)S(1)} %pad_maximum_fusion.4), channel_id=1, source_target_pairs={{1,0},{2,1},{3,2},{4,3},{5,4},{6,5},{7,6},{8,7},{9,8},{10,9},{11,1... | collective-permute-start | bytes 18440 | tf_op jit(solution)/shard_map/ppermute | solution.py:21
  24.7 8.4 %collective-permute-start.2 = (f32[3,1,4,128]{3,2,1,0:T(4,128)S(1)}, f32[3,1,4,128]{3,2,1,0:T(4,128)S(1)}, u32[]{:S(2)}, u32[]{:S(2)}) collective-permute-start(f32[3,1,4,128]{3,2,1,0:T(4,128)S(1)} %pad_maximum_fusion.4), channel_id=1, source_target_pairs={{0,1},{1,2},{2,3},{3,4},{4,5},{5,6},{6,7},{7,8},{8,9},{9,10},{10,1... | collective-permute-start | bytes 18440 | tf_op jit(solution)/shard_map/ppermute | solution.py:20
  24.9 14.4 %copy-start.74 = (f32[8]{0:T(128)}, f32[8]{0:T(128)S(1)}, u32[]{:S(2)}) copy-start(f32[8]{0:T(128)S(1)} %add_multiply_fusion) | copy-start | bytes 100
  34.3 5.0 %copy-start.56 = (pred[256,5]{1,0:T(32,128)(4,1)}, pred[256,5]{1,0:T(32,128)(4,1)S(1)}, u32[]{:S(2)}) copy-start(pred[256,5]{1,0:T(32,128)(4,1)S(1)} %gather_fusion.8) | copy-start | bytes 3844
  35.1 4.2 %copy-start.58 = (pred[256,5]{1,0:T(32,128)(4,1)}, pred[256,5]{1,0:T(32,128)(4,1)S(1)}, u32[]{:S(2)}) copy-start(pred[256,5]{1,0:T(32,128)(4,1)S(1)} %gather_fusion.7) | copy-start | bytes 3844
  35.5 3.9 %copy-start.4 = (f32[2,512,64]{1,2,0:T(8,128)S(1)}, f32[2,512,64]{1,2,0:T(8,128)}, u32[]{:S(2)}) copy-start(f32[2,512,64]{1,2,0:T(8,128)} %param.33) | copy-start | bytes 786436
  37.2 2.9 copy-start.65
  37.8 2.3 copy-start.60
  37.8 7.3 %copy-start.51 = (f32[256]{0:T(256)}, f32[256]{0:T(256)S(1)}, u32[]{:S(2)}) copy-start(f32[256]{0:T(256)S(1)} %get-tuple-element.151) | copy-start | bytes 3076
  37.8 8.5 %copy-start.42 = (f32[3,256]{1,0:T(4,128)}, f32[3,256]{1,0:T(4,128)S(1)}, u32[]{:S(2)}) copy-start(f32[3,256]{1,0:T(4,128)S(1)} %bitcast_divide_fusion) | copy-start | bytes 9220
  39.0 2.3 copy-start.1
  40.1 65.5 %copy-start.29 = (f32[256,64]{0,1:T(8,128)}, f32[256,64]{0,1:T(8,128)S(1)}, u32[]{:S(2)}) copy-start(f32[256,64]{0,1:T(8,128)S(1)} %get-tuple-element.155) | copy-start | bytes 196612
  41.2 2.3 copy-start.37
  43.5 3.7 %copy-start.27 = (s32[1,1,256]{2,1,0:T(1,128)S(1)}, s32[1,1,256]{2,1,0:T(1,128)}, u32[]{:S(2)}) copy-start(s32[1,1,256]{2,1,0:T(1,128)} %param.26) | copy-start | bytes 3076
  46.3 6.0 %copy-start.52 = (f32[256]{0:T(256)S(1)}, f32[256]{0:T(256)}, u32[]{:S(2)}) copy-start(f32[256]{0:T(256)} %copy-done.51) | copy-start | bytes 3076
  46.3 6.0 %copy-start.72 = (f32[512]{0:T(512)S(1)}, f32[512]{0:T(512)}, u32[]{:S(2)}) copy-start(f32[512]{0:T(512)} %param.35) | copy-start | bytes 6148
  57.7 2.2 copy-start.38
  57.7 2.2 copy-start.61
  57.7 2.2 copy-start.69
  57.8 2.2 copy-start.75
  60.0 33.7 %copy-start.77 = (f32[3,1,1,128]{3,2,1,0:T(1,128)S(1)}, f32[3,1,1,128]{3,2,1,0:T(1,128)}, u32[]{:S(2)}) copy-start(f32[3,1,1,128]{3,2,1,0:T(1,128)} %param.29) | copy-start | bytes 4612
  64.1 31.8 %slice-start = ((f32[3,1280]{0,1:T(8,128)}), f32[3,128]{0,1:T(8,128)S(1)}, s32[]{:S(2)}) async-start(f32[3,1280]{0,1:T(8,128)} %scatter_custom_fusion), calls=%async_computation.1 | async-start | bytes 131072 | tf_op jit(solution)/shard_map/slice | solution.py:154
  66.1 57.5 %copy-start.62 = (f32[256]{0:T(256)S(1)}, f32[256]{0:T(256)}, u32[]{:S(2)}) copy-start(f32[256]{0:T(256)} %copy-done.60) | copy-start | bytes 3076
  66.1 57.5 %copy-start.70 = (f32[256]{0:T(256)S(1)}, f32[256]{0:T(256)}, u32[]{:S(2)}) copy-start(f32[256]{0:T(256)} %get-tuple-element.152) | copy-start | bytes 3076
  66.2 57.5 %copy-start.76 = (f32[8]{0:T(128)S(1)}, f32[8]{0:T(128)}, u32[]{:S(2)}) copy-start(f32[8]{0:T(128)} %copy-done.74) | copy-start | bytes 100
  66.2 9.7 %collective-permute-start.4 = (f32[3,128]{0,1:T(8,128)S(1)}, f32[3,128]{0,1:T(8,128)}, u32[]{:S(2)}, u32[]{:S(2)}) collective-permute-start(f32[3,128]{0,1:T(8,128)S(1)} %get-tuple-element.114), channel_id=1, source_target_pairs={{0,31},{1,0},{2,1},{3,2},{4,3},{5,4},{6,5},{7,6},{8,7},{9,8},{10,9... | collective-permute-start | bytes 4616 | tf_op jit(solution)/shard_map/ppermute | solution.py:28
  66.2 16.8 %collective-permute-start.14 = (f32[3,128]{0,1:T(8,128)S(1)}, f32[3,128]{0,1:T(8,128)}, u32[]{:S(2)}, u32[]{:S(2)}) collective-permute-start(f32[3,128]{0,1:T(8,128)S(1)} %get-tuple-element.115), channel_id=1, source_target_pairs={{0,1},{1,2},{2,3},{3,4},{4,5},{5,6},{6,7},{7,8},{8,9},{9,10},{10,1... | collective-permute-start | bytes 4616 | tf_op jit(solution)/shard_map/ppermute | solution.py:28
  69.2 13.9 %collective-permute-start.13 = (f32[3,128]{0,1:T(8,128)S(1)}, f32[3,128]{0,1:T(8,128)S(1)}, u32[]{:S(2)}, u32[]{:S(2)}) collective-permute-start(f32[3,128]{0,1:T(8,128)S(1)} %get-tuple-element.116), channel_id=1, source_target_pairs={{0,32},{32,64},{64,96},{96,0},{1,33},{33,65},{65,97},{97,1},{2,34}... | collective-permute-start | bytes 4616 | tf_op jit(solution)/shard_map/ppermute | solution.py:28
  71.3 12.3 %collective-permute-start.11 = (f32[3,128]{0,1:T(8,128)S(1)}, f32[3,128]{0,1:T(8,128)}, u32[]{:S(2)}, u32[]{:S(2)}) collective-permute-start(f32[3,128]{0,1:T(8,128)S(1)} %get-tuple-element.117), channel_id=1, source_target_pairs={{0,31},{1,0},{2,1},{3,2},{4,3},{5,4},{6,5},{7,6},{8,7},{9,8},{10,9... | collective-permute-start | bytes 4616 | tf_op jit(solution)/shard_map/ppermute | solution.py:28
  75.9 9.5 %collective-permute-start.10 = (f32[3,128]{0,1:T(8,128)S(1)}, f32[3,128]{0,1:T(8,128)S(1)}, u32[]{:S(2)}, u32[]{:S(2)}) collective-permute-start(f32[3,128]{0,1:T(8,128)S(1)} %get-tuple-element.118), channel_id=1, source_target_pairs={{0,1},{1,2},{2,3},{3,4},{4,5},{5,6},{6,7},{7,8},{8,9},{9,10},{10,1... | collective-permute-start | bytes 4616 | tf_op jit(solution)/shard_map/ppermute | solution.py:28
  75.9 10.3 %collective-permute-start.9 = (f32[3,128]{0,1:T(8,128)S(1)}, f32[3,128]{0,1:T(8,128)S(1)}, u32[]{:S(2)}, u32[]{:S(2)}) collective-permute-start(f32[3,128]{0,1:T(8,128)S(1)} %get-tuple-element.119), channel_id=1, source_target_pairs={{0,31},{1,0},{2,1},{3,2},{4,3},{5,4},{6,5},{7,6},{8,7},{9,8},{10,9... | collective-permute-start | bytes 4616 | tf_op jit(solution)/shard_map/ppermute | solution.py:28
  83.1 8.9 %collective-permute-start.7 = (f32[3,128]{0,1:T(8,128)S(1)}, f32[3,128]{0,1:T(8,128)}, u32[]{:S(2)}, u32[]{:S(2)}) collective-permute-start(f32[3,128]{0,1:T(8,128)S(1)} %get-tuple-element.120), channel_id=1, source_target_pairs={{0,1},{1,2},{2,3},{3,4},{4,5},{5,6},{6,7},{7,8},{8,9},{9,10},{10,1... | collective-permute-start | bytes 4616 | tf_op jit(solution)/shard_map/ppermute | solution.py:28
  83.1 10.6 %collective-permute-start.6 = (f32[3,128]{0,1:T(8,128)S(1)}, f32[3,128]{0,1:T(8,128)S(1)}, u32[]{:S(2)}, u32[]{:S(2)}) collective-permute-start(f32[3,128]{0,1:T(8,128)S(1)} %get-tuple-element.121), channel_id=1, source_target_pairs={{0,96},{32,0},{64,32},{96,64},{1,97},{33,1},{65,33},{97,65},{2,98}... | collective-permute-start | bytes 4616 | tf_op jit(solution)/shard_map/ppermute | solution.py:28
  83.6 10.1 %collective-permute-start.5 = (f32[3,128]{0,1:T(8,128)}, f32[3,128]{0,1:T(8,128)S(1)}, u32[]{:S(2)}, u32[]{:S(2)}) collective-permute-start(f32[3,128]{0,1:T(8,128)} %collective-permute-done.4), channel_id=1, source_target_pairs={{0,96},{32,0},{64,32},{96,64},{1,97},{33,1},{65,33},{97,65},{2,98}... | collective-permute-start | bytes 4616 | tf_op jit(solution)/shard_map/ppermute | solution.py:28
  85.4 8.3 %collective-permute-start.15 = (f32[3,128]{0,1:T(8,128)}, f32[3,128]{0,1:T(8,128)S(1)}, u32[]{:S(2)}, u32[]{:S(2)}) collective-permute-start(f32[3,128]{0,1:T(8,128)} %collective-permute-done.14), channel_id=1, source_target_pairs={{0,32},{32,64},{64,96},{96,0},{1,33},{33,65},{65,97},{97,1},{2,34}... | collective-permute-start | bytes 4616 | tf_op jit(solution)/shard_map/ppermute | solution.py:28
  86.2 7.6 %collective-permute-start.12 = (f32[3,128]{0,1:T(8,128)}, f32[3,128]{0,1:T(8,128)S(1)}, u32[]{:S(2)}, u32[]{:S(2)}) collective-permute-start(f32[3,128]{0,1:T(8,128)} %collective-permute-done.11), channel_id=1, source_target_pairs={{0,32},{32,64},{64,96},{96,0},{1,33},{33,65},{65,97},{97,1},{2,34}... | collective-permute-start | bytes 4616 | tf_op jit(solution)/shard_map/ppermute | solution.py:28
  92.0 3.9 %collective-permute-start.8 = (f32[3,128]{0,1:T(8,128)}, f32[3,128]{0,1:T(8,128)S(1)}, u32[]{:S(2)}, u32[]{:S(2)}) collective-permute-start(f32[3,128]{0,1:T(8,128)} %collective-permute-done.7), channel_id=1, source_target_pairs={{0,96},{32,0},{64,32},{96,64},{1,97},{33,1},{65,33},{97,65},{2,98}... | collective-permute-start | bytes 4616 | tf_op jit(solution)/shard_map/ppermute | solution.py:28
  98.4 3.8 %collective-permute-start.17 = (f32[1,1,3,128]{2,3,1,0:T(8,128)S(1)}, f32[1,1,3,128]{2,3,1,0:T(8,128)S(1)}, u32[]{:S(2)}, u32[]{:S(2)}) collective-permute-start(f32[1,1,3,128]{2,3,1,0:T(8,128)S(1)} %bitcast.553), channel_id=1, source_target_pairs={{32,0},{64,32},{96,64},{0,96},{33,1},{65,33},{97,65},{1,97},{34,2}... | collective-permute-start | bytes 4616 | tf_op jit(solution)/shard_map/ppermute | solution.py:21
  98.4 3.7 %collective-permute-start.16 = (f32[1,1,3,128]{2,3,1,0:T(8,128)S(1)}, f32[1,1,3,128]{2,3,1,0:T(8,128)S(1)}, u32[]{:S(2)}, u32[]{:S(2)}) collective-permute-start(f32[1,1,3,128]{2,3,1,0:T(8,128)S(1)} %bitcast.554), channel_id=1, source_target_pairs={{0,32},{32,64},{64,96},{96,0},{1,33},{33,65},{65,97},{97,1},{2,34}... | collective-permute-start | bytes 4616 | tf_op jit(solution)/shard_map/ppermute | solution.py:20
  102.1 6.2 %collective-permute-start.19 = (f32[3,1,3,128]{2,3,1,0:T(8,128)S(1)}, f32[3,1,3,128]{2,3,1,0:T(8,128)}, u32[]{:S(2)}, u32[]{:S(2)}) collective-permute-start(f32[3,1,3,128]{2,3,1,0:T(8,128)S(1)} %pad_maximum_fusion.2), channel_id=1, source_target_pairs={{1,0},{2,1},{3,2},{4,3},{5,4},{6,5},{7,6},{8,7},{9,8},{10,9},{11,1... | collective-permute-start | bytes 13832 | tf_op jit(solution)/shard_map/ppermute | solution.py:21
  105.0 11.3 %collective-permute-start.18 = (f32[3,1,3,128]{2,3,1,0:T(8,128)S(1)}, f32[3,1,3,128]{2,3,1,0:T(8,128)S(1)}, u32[]{:S(2)}, u32[]{:S(2)}) collective-permute-start(f32[3,1,3,128]{2,3,1,0:T(8,128)S(1)} %pad_maximum_fusion.2), channel_id=1, source_target_pairs={{0,1},{1,2},{2,3},{3,4},{4,5},{5,6},{6,7},{7,8},{8,9},{9,10},{10,1... | collective-permute-start | bytes 13832 | tf_op jit(solution)/shard_map/ppermute | solution.py:20
  117.5 8.8 %copy-start.30 = (f32[256,64]{0,1:T(8,128)S(1)}, f32[256,64]{0,1:T(8,128)}, u32[]{:S(2)}) copy-start(f32[256,64]{0,1:T(8,128)} %copy-done.29) | copy-start | bytes 196612
  117.5 8.8 %copy-start.53 = (f32[256]{0:T(256)S(1)}, f32[256]{0:T(256)}, u32[]{:S(2)}) copy-start(f32[256]{0:T(256)} %copy-done.51) | copy-start | bytes 3076
  119.5 7.5 %copy-start.44 = (f32[3,256]{1,0:T(4,128)S(1)}, f32[3,256]{1,0:T(4,128)}, u32[]{:S(2)}) copy-start(f32[3,256]{1,0:T(4,128)} %copy-done.42) | copy-start | bytes 9220
  119.5 7.5 %copy-start.28 = (s32[1,1,256]{2,1,0:T(1,128)S(1)}, s32[1,1,256]{2,1,0:T(1,128)}, u32[]{:S(2)}) copy-start(s32[1,1,256]{2,1,0:T(1,128)} %param.26) | copy-start | bytes 3076
  131.1 2.5 copy-start.5
  136.8 7.2 %copy-start.73 = (f32[512]{0:T(512)S(1)}, f32[512]{0:T(512)}, u32[]{:S(2)}) copy-start(f32[512]{0:T(512)} %param.35) | copy-start | bytes 6148
  139.9 4.1 %copy-start.3 = (f32[512,256]{0,1:T(8,128)S(1)}, f32[512,256]{0,1:T(8,128)}, u32[]{:S(2)}) copy-start(f32[512,256]{0,1:T(8,128)} %copy-done.2) | copy-start | bytes 1572868
  148.5 2.3 copy-start.13
  148.5 2.3 copy-start.15
  148.5 2.3 copy-start.22
  148.5 2.3 copy-start.25
  154.2 2.7 copy-start.40
  170.3 2.2 copy-start.59
  (42 other events, 59.7 us)
Sparse Core Ops, SparseCore 0:
  170.4 149.3 all-reduce.13
where the time goes:
time: 335 us; the launch traced here: 332 us
  waiting for transfers between devices  109 us (33%)
  blocking collectives  65 us (19%)
  matrix products  60.4 us (18%)
  starting transfers between devices  37 us (11%)
  local copies, waits for them, and re-layouts  26.1 us (8%)
  other arithmetic  18.2 us (5%)
  between operations  16.7 us (5%)
    psum x1, waiting for transfers between devices, on_device(): grads = lax.psum(local, ('slab', 'brick'))  80.7 us
    psum x1, blocking collectives, on_device(): grads = lax.psum(local, ('slab', 'brick'))  65 us
    dot_general x82, matrix products, product(): jnp.dot(left, right, precision=lax.Precision.HIGHEST, preferred_element_t...  60.4 us
    ppermute x12, starting transfers between devices, passed_along(): lax.ppermute(x, axis, [(i, (i + by) % devices) for i in range(devices)])  20.2 us
    ppermute x4, waiting for transfers between devices, with_halo(): before = lax.ppermute(last, axis, up)  14.4 us
    ppermute x4, starting transfers between devices, with_halo(): after = lax.ppermute(initial, axis, down)  13 us
    unnamed x173, local copies, waits for them, and re-layouts  10.9 us
    ppermute x12, waiting for transfers between devices, passed_along(): lax.ppermute(x, axis, [(i, (i + by) % devices) for i in range(devices)])  9.44 us
  transfers between devices with their start and end apart: 21, of which 8 were waited for; matrix products, arithmetic and copies ran while one was open for 2% of the time, Pallas kernels for 0%

commit v1 on v0

v1 whole, which is shorter than its diff:
```python
import math

import jax
import jax.numpy as jnp
from jax import lax
from jax.experimental import pallas as pl
from jax.experimental.pallas import tpu as pltpu
from jax.sharding import PartitionSpec as P

F32 = jnp.float32
BF16 = jnp.bfloat16
MESH = pl.DeviceIdType.MESH
VMEM = pltpu.VMEM
NN = (((1,), (0,)), ((), ()))
NT = (((1,), (1,)), ((), ()))
TN = (((0,), (0,)), ((), ()))

cell_width = 1.75
cutoff_radius = 6.0
softening = 0.25

N_SLAB, N_BRICK = 4, 32
H, M, E, ATOMS = 512, 64, 256, 128
ROWS = (576, 768)
PARTS = ((192, 192, 192), (256, 256, 256))
ORDERS = (("x", "y", "z"), ("y", "z", "x"), ("z", "x", "y"))
NEIGHBOURS = [(p, q) for p in range(3) for q in range(3) if (p, q) != (1, 1)]


def dot(a, b, dims=NN):
    return lax.dot_general(a, b, dims, preferred_element_type=F32)


def split(x):
    high = x.astype(BF16)
    return high, (x - high.astype(F32)).astype(BF16)


def mm3(a, b, dims=NN):
    return dot(a[0], b[0], dims) + (dot(a[0], b[1], dims) + dot(a[1], b[0], dims))


def mm2(a, exact, dims=NN):
    return dot(a[0], exact, dims) + dot(a[1], exact, dims)


def pieces(x):
    a = x.astype(BF16).astype(F32)
    b = (x - a).astype(BF16).astype(F32)
    c = (x - a) - b
    return jnp.concatenate([a, b, c, jnp.zeros_like(x)], axis=0).astype(BF16)


def select(x, hot, dims=NN):
    r = dot(pieces(x), hot, dims)
    return (r[0:8] + r[8:16]) + r[16:24]


def onehot(values, count):
    ids = lax.broadcasted_iota(jnp.int32, (count, values.shape[1]), 0)
    return jnp.where(ids == values, 1.0, 0.0).astype(BF16)


def padded(x):
    return jnp.concatenate([x, jnp.zeros((M, x.shape[1]), x.dtype)], axis=0)


def padded2(x):
    return padded(x[0]), padded(x[1])


def sigmoid(x):
    return 1.0 / (1.0 + jnp.exp(-x))


def device_at(core, x, y, z):
    return (lax.rem(x, 2) * 2 + core, (z * 4 + y) * 2 + lax.div(x, 2))


def kernel(
    pos_ref, spec_ref, exp_ref, cen_ref, nbr_ref, cnt_ref, tgt_ref, rad_ref, cem_ref, nem_ref, ow_ref, env_hbm, lat_hbm,
    forces_ref, g1_ref, g2_ref,
    w_lat, w_env, latT, latN, envT, envN, a0, oc,
    tbl, ttbl, sendbuf, gsend, grecv,
    lat, xh, xl, dh, dl, sp, spp, dlat, osum, tt, pp, uu,
    h1, h2, c1, c2, ra1, ra2, rb1, rb2, rc1, rc2,
    wsem, hs, hr, ars, arr,
):
    s, b = lax.axis_index("slab"), lax.axis_index("brick")
    core, x = lax.rem(s, 2), 2 * lax.rem(b, 2) + lax.div(s, 2)
    y, z = lax.rem(lax.div(b, 2), 4), lax.div(b, 8)
    at = {"x": x, "y": y, "z": z}
    partner = device_at(1 - core, x, y, z)

    def peer(axis, k):
        c = dict(at)
        c[axis] = lax.rem(c[axis] + k, 4)
        return device_at(core, c["x"], c["y"], c["z"])

    def around(p, q):
        return (lax.rem(s + p + N_SLAB - 1, N_SLAB), lax.rem(b + q + N_BRICK - 1, N_BRICK))

    barrier = pltpu.get_barrier_semaphore()
    everyone = [around(p, q) for p, q in NEIGHBOURS] + [partner] + [peer(a, k) for a in "xyz" for k in (1, 2, 3)]
    for d in everyone:
        pl.semaphore_signal(barrier, inc=1, device_id=d, device_id_type=MESH)

    loads = [
        pltpu.make_async_copy(env_hbm, w_env, wsem.at[0]),
        pltpu.make_async_copy(lat_hbm, w_lat, wsem.at[1]),
    ]
    for c in loads:
        c.start()

    tbl[0] = jnp.zeros((8, ATOMS), F32)
    for m in range(3):
        tbl[0, m : m + 1, :] = pos_ref[m, 0]
    tbl[0, 3:4, :] = spec_ref[0].astype(F32)
    hot_exp = onehot(exp_ref[0], ATOMS)
    sendbuf[0] = select(tbl[0], hot_exp)

    pl.semaphore_wait(barrier, len(everyone))

    def halo(stage, sources, lands, back):
        out = []
        for i, (p, q) in enumerate(NEIGHBOURS):
            k = 3 * p + q
            to = around(p, q) if back else around(2 - p, 2 - q)
            out.append(
                pltpu.make_async_remote_copy(
                    src_ref=sources(k), dst_ref=lands(k), send_sem=hs.at[stage, i], recv_sem=hr.at[stage, i],
                    device_id=to, device_id_type=MESH,
                )
            )
        for c in out:
            c.start()
        return out

    sends = []
    first = halo(0, lambda k: sendbuf.at[0], lambda k: tbl.at[1 + k], False)
    sends += first

    tbl[5] = sendbuf[0]
    center = cen_ref[0]
    hot_c = onehot(center, ATOMS)
    hot_n = onehot(nbr_ref[0], 10 * ATOMS)
    same = dot(hot_c, hot_c, TN).astype(BF16)
    lane = lax.broadcasted_iota(jnp.int32, (1, E), 1)
    live = jnp.where(lane < cnt_ref[...], 1.0, 0.0)
    o_col = jnp.transpose(jnp.broadcast_to(ow_ref[...], (128, H)))
    oc[...] = jnp.concatenate([o_col, o_col], axis=1)
    a0[...] = jnp.zeros_like(a0)
    a0[0:8] = rad_ref[...]
    a0[8:13] = cem_ref[...]
    a0[16:21] = nem_ref[...]
    a0s = split(a0[...])
    for c in loads:
        c.wait()
    for l in range(2):
        w = w_lat[l]
        latN[l, 0], latN[l, 1] = split(w)
        latT[l, 0], latT[l, 1] = split(jnp.transpose(padded(w)))
        w = w_env[l]
        envT[l, 0], envT[l, 1] = split(w)
        envN[l, 0], envN[l, 1] = split(jnp.transpose(padded(w)))

    pc = select(tbl[0], hot_c)

    for c in first:
        c.wait_recv()

    row = lax.broadcasted_iota(jnp.int32, (8, 1), 0)
    blocks = [tbl[0]]
    for p in range(3):
        for q in range(3):
            t = tbl[1 + 3 * p + q]
            if (p, q) != (1, 1):
                cross_z = (lax.div(s + p - 1 + N_SLAB, N_SLAB) - 1).astype(F32) * (N_SLAB * cell_width)
                cross_y = (lax.div(b + q - 1 + N_BRICK, N_BRICK) - 1).astype(F32) * (N_BRICK * cell_width)
                t = t + jnp.where(row == 2, cross_z, 0.0) + jnp.where(row == 1, cross_y, 0.0)
            blocks.append(t)
    pn = select(jnp.concatenate(blocks, axis=1), hot_n)
    vec = jnp.where(row < 3, pn - pc, 0.0)
    squared = jnp.sum(vec * vec, axis=0, keepdims=True) + softening
    dist = jnp.sqrt(squared)
    inv_d = 1.0 / dist
    base = 1.0 - squared / (cutoff_radius * cutoff_radius)
    env = base * base * live
    direction = vec * inv_d
    order = (row + 1).astype(F32) * (math.pi / cutoff_radius)
    angle = order * dist
    sine, cosine = jnp.sin(angle), jnp.cos(angle)
    basis = sine * inv_d
    basis_d = (order * cosine - basis) * inv_d
    hot_sc = jnp.where(row.astype(F32) == pc[3:4], 1.0, 0.0)
    hot_sn = jnp.where(row.astype(F32) == pn[3:4], 1.0, 0.0)
    feats = jnp.concatenate([basis, hot_sc, hot_sn, jnp.zeros((8, E), F32)], axis=0)

    def activation(i, value):
        g = sigmoid(value)
        sp[i] = g * (1.0 + value * (1.0 - g))
        spp[i] = (g * (1.0 - g)) * (2.0 + value * (1.0 - 2.0 * g))
        return value * g

    def keep_x(l, half, rows, value):
        high, low = split(value)
        lanes = slice(E * half, E * half + E)
        xh[l, rows, lanes] = high
        xl[l, rows, lanes] = low
        return high, low

    def keep_d(l, half, value):
        high, low = split(value)
        lanes = slice(E * half, E * half + E)
        dh[l, :, lanes] = high
        dl[l, :, lanes] = low
        return high, low

    def thirds(v):
        return [v[m * M : m * M + M] for m in range(3)]

    def outer(d, w):
        return jnp.concatenate([d[m : m + 1] * w for m in range(3)], axis=0)

    def with_same(t):
        return mm2(split(t), same)

    def dotted(a, c):
        r = a * c
        return (r[0:M] + r[M : 2 * M]) + r[2 * M :]

    lat[0] = activation(0, mm3(a0s, split(feats), TN))
    for l in range(2):
        now = keep_x(l, 1, slice(0, H), lat[l])
        u = mm3((envT[l, 0], envT[l, 1]), now)
        uu[l] = u
        t = outer(direction, u * env)
        tt[l] = t
        pr = with_same(t)
        pp[l] = pr
        inv = keep_x(l, 1, slice(H, H + M), dotted(t, pr))
        update = mm3((latT[l, 0, :, 0:H], latT[l, 1, :, 0:H]), now) + mm3((latT[l, 0, :, H:], latT[l, 1, :, H:]), padded2(inv))
        lat[l + 1] = lat[l] + activation(l + 1, update)

    d_env = jnp.sum(oc[...] * lat[2], axis=0, keepdims=True)
    d_dir = [jnp.zeros((1, E), F32) for _ in range(3)]
    dlat[2] = oc[...] * env
    kept = [None, None]
    for l in (1, 0):
        delta = keep_d(l, 0, dlat[l + 1] * sp[l + 1])
        d_inv = mm3((latN[l, 0, H:], latN[l, 1, H:]), delta)
        d_inv3 = jnp.concatenate([d_inv] * 3, axis=0)
        d_t = d_inv3 * pp[l] + with_same(d_inv3 * tt[l])
        w = uu[l] * env
        d_w = dotted(outer(direction, jnp.ones((M, E), F32)), d_t)
        for m, part in enumerate(thirds(d_t)):
            d_dir[m] += jnp.sum(part * w, axis=0, keepdims=True)
        d_env += jnp.sum(d_w * uu[l], axis=0, keepdims=True)
        d_u = split(d_w * env)
        kept[l] = (d_inv3, d_t, d_w, d_u)
        back = mm3((latN[l, 0, 0:H], latN[l, 1, 0:H]), delta) + mm3((envN[l, 0], envN[l, 1]), padded2(d_u))
        dlat[l] = dlat[l + 1] + back
    delta0 = keep_d(2, 0, dlat[0] * sp[0])
    d_basis = mm3(a0s, delta0)[0:8]
    d_dir8 = jnp.concatenate(d_dir + [jnp.zeros((5, E), F32)], axis=0)
    d_dist = jnp.sum(d_basis * basis_d, axis=0, keepdims=True) - jnp.sum(d_dir8 * direction, axis=0, keepdims=True) * inv_d
    base_d = (-2.0 / (cutoff_radius * cutoff_radius)) * base * live
    d_squared = d_env * base_d + d_dist * (0.5 * inv_d)
    d_vec = d_dir8 * inv_d + 2.0 * vec * d_squared
    d_table = select(d_vec, hot_n, NT)
    own = d_table[:, 0:ATOMS] - select(d_vec, hot_c, NT)
    for k in range(9):
        gsend[k] = d_table[:, ATOMS * (k + 1) : ATOMS * (k + 2)]
    second = halo(1, lambda k: gsend.at[k], lambda k: grecv.at[k], True)
    sends += second
    for c in second:
        c.wait_recv()
    returned = gsend[4]
    for p, q in NEIGHBOURS:
        returned = returned + grecv[3 * p + q]
    total = own + select(returned, hot_exp, NT)
    ttbl[0] = jnp.zeros((8, ATOMS), F32)
    for m in range(3):
        forces_ref[m, 0] = -total[m : m + 1]
        ttbl[0, m : m + 1, :] = (2.0 / (3.0 * ATOMS)) * (total[m : m + 1] + tgt_ref[m, 0])

    sendbuf[1] = select(ttbl[0], hot_exp)
    third = halo(2, lambda k: sendbuf.at[1], lambda k: ttbl.at[1 + k], False)
    sends += third
    ttbl[5] = sendbuf[1]
    vc = select(ttbl[0], hot_c)
    for c in third:
        c.wait_recv()
    vn = select(jnp.concatenate([ttbl[k] for k in range(10)], axis=1), hot_n)
    vec_t = vn - vc
    dist_t = jnp.sum(vec * vec_t, axis=0, keepdims=True) * inv_d
    env_t = (2.0 * base_d) * (dist * dist_t)
    dir_t = (vec_t - direction * dist_t) * inv_d
    basis_t = basis_d * dist_t
    feats_t = jnp.concatenate([basis_t, jnp.zeros((24, E), F32)], axis=0)

    first_t = mm3(a0s, split(feats_t), TN)
    lat_t = sp[0] * first_t
    kept_t = [None, None]
    update_t = [None, None]
    for l in range(2):
        now = keep_x(l, 0, slice(0, H), lat_t)
        u_t = mm3((envT[l, 0], envT[l, 1]), now)
        w = uu[l] * env
        w_t = u_t * env + uu[l] * env_t
        t_t = outer(dir_t, w) + outer(direction, w_t)
        pr_t = with_same(t_t)
        inv_t = keep_x(l, 0, slice(H, H + M), dotted(t_t, pp[l]) + dotted(tt[l], pr_t))
        kept_t[l] = (t_t, pr_t)
        update_t[l] = mm3((latT[l, 0, :, 0:H], latT[l, 1, :, 0:H]), now) + mm3((latT[l, 0, :, H:], latT[l, 1, :, H:]), padded2(inv_t))
        lat_t = lat_t + sp[l + 1] * update_t[l]

    half = (h1, h2)
    from_core = (c1, c2)
    from_a, from_b, from_c = (ra1, ra2), (rb1, rb2), (rc1, rc2)
    result = (g1_ref, g2_ref)
    flying = {}

    def place(g, i):
        n = PARTS[g][i]
        row0 = sum(PARTS[g][:i])
        a, bb, c = ORDERS[i]
        row_a = row0 + at[a] * (n // 4)
        row_b = row_a + lax.div(at[bb], 2) * (n // 8)
        return n, row0, a, bb, c, pl.multiple_of(row_a, 8), pl.multiple_of(row_b, 8)

    def piece_of(row_a, n, where):
        rows = pl.ds(pl.multiple_of(row_a + lax.div(where, 2) * (n // 8), 8), n // 8)
        return rows, lax.rem(where, 2) * 128

    def copy(g, i, j, src, dst, to):
        c = pltpu.make_async_remote_copy(
            src_ref=src, dst_ref=dst, send_sem=ars.at[g, i, j], recv_sem=arr.at[g, i, j], device_id=to, device_id_type=MESH
        )
        c.start()
        sends.append(c)
        flying[g, i, j] = c

    def lands(g, i, j):
        flying[g, i, j].wait_recv()

    def lanes_at(first, count=128):
        return pl.ds(pl.multiple_of(first, 128), count)

    def start_core(g, i):
        n, row0, *_ = place(g, i)
        copy(g, i, 0, half[g].at[0, row0 : row0 + n], from_core[g].at[row0 : row0 + n], partner)

    def core_to_a(g, i):
        n, row0, a, *_ = place(g, i)
        lands(g, i, 0)
        rows = slice(row0, row0 + n)
        half[g][1, rows] = half[g][1, rows] + from_core[g][rows]
        for k in (1, 2, 3):
            theirs = row0 + lax.rem(at[a] + k, 4) * (n // 4)
            copy(g, i, k, half[g].at[1, pl.ds(pl.multiple_of(theirs, 8), n // 4)], from_a[g].at[i, k - 1], peer(a, k))

    def a_to_b(g, i):
        n, row0, a, bb, c, row_a, row_b = place(g, i)
        for k in (1, 2, 3):
            lands(g, i, k)
        rows = pl.ds(row_a, n // 4)
        half[g][1, rows] = (half[g][1, rows] + from_a[g][i, 1]) + (from_a[g][i, 0] + from_a[g][i, 2])
        for k in (1, 2, 3):
            rows, lane0 = piece_of(row_a, n, lax.rem(at[bb] + k, 4))
            copy(g, i, 3 + k, half[g].at[1, rows, lanes_at(lane0)], from_b[g].at[i, k - 1], peer(bb, k))

    def b_to_c(g, i):
        n, row0, a, bb, c, row_a, row_b = place(g, i)
        for k in (1, 2, 3):
            lands(g, i, 3 + k)
        rows, lane0 = piece_of(row_a, n, at[bb])
        lanes = lanes_at(lane0)
        half[g][1, rows, lanes] = (half[g][1, rows, lanes] + from_b[g][i, 1]) + (from_b[g][i, 0] + from_b[g][i, 2])
        for k in (1, 2, 3):
            copy(g, i, 6 + k, half[g].at[1, rows, lanes], from_c[g].at[i, k - 1], peer(c, k))

    def c_to_b(g, i):
        n, row0, a, bb, c, row_a, row_b = place(g, i)
        for k in (1, 2, 3):
            lands(g, i, 6 + k)
        rows, lane0 = piece_of(row_a, n, at[bb])
        mine = half[g][1, rows, lanes_at(lane0)]
        out = lanes_at(core * 256 + lane0)
        result[g][rows, out] = (mine + from_c[g][i, 1]) + (from_c[g][i, 0] + from_c[g][i, 2])
        for k in (1, 2, 3):
            here = result[g].at[rows, out]
            copy(g, i, 9 + k, here, here, peer(bb, k))

    def b_to_a(g, i):
        n, row0, a, bb, c, row_a, row_b = place(g, i)
        for k in (1, 2, 3):
            lands(g, i, 9 + k)
        here = result[g].at[pl.ds(row_a, n // 4), lanes_at(core * 256, 256)]
        for k in (1, 2, 3):
            copy(g, i, 12 + k, here, here, peer(a, k))

    def a_to_core(g, i):
        n, row0, *_ = place(g, i)
        for k in (1, 2, 3):
            lands(g, i, 12 + k)
        here = result[g].at[row0 : row0 + n, lanes_at(core * 256, 256)]
        copy(g, i, 16, here, here, partner)

    def finish(g, i):
        lands(g, i, 16)

    def step(g, f):
        for i in range(3):
            f(g, i)

    def gradient(l, h):
        rows = pl.ds(pl.multiple_of(h * 256, 256), 256)
        return mm3((xh[l], xl[l]), (dh[l, rows], dl[l, rows]), NT)

    lat2_t = lat_t
    scaled = oc[...] * env_t
    delta_t = keep_d(1, 1, scaled * sp[2] + dlat[2] * (spp[2] * update_t[1]))
    h1[0] = gradient(1, 1 - core)
    step(0, start_core)
    h1[1] = gradient(1, core)

    dlat_t = scaled
    env_rows = [None, None]
    for l in (1, 0):
        if l == 0:
            delta_t = keep_d(0, 1, dlat_t * sp[1] + dlat[1] * (spp[1] * update_t[0]))
            step(0, core_to_a)
        d_inv_t = mm3((latN[l, 0, H:], latN[l, 1, H:]), delta_t)
        d_inv3, d_t, d_w, d_u = kept[l]
        t_t, pr_t = kept_t[l]
        d_inv3_t = jnp.concatenate([d_inv_t] * 3, axis=0)
        d_t_t = d_inv3_t * pp[l] + d_inv3 * pr_t + with_same(d_inv3_t * tt[l] + d_inv3 * t_t)
        ones = jnp.ones((M, E), F32)
        d_w_t = dotted(outer(dir_t, ones), d_t) + dotted(outer(direction, ones), d_t_t)
        d_u_t = split(d_w_t * env + d_w * env_t)
        env_rows[l] = (jnp.concatenate([d_u[0], d_u_t[0]], axis=1), jnp.concatenate([d_u[1], d_u_t[1]], axis=1))
        back = mm3((latN[l, 0, 0:H], latN[l, 1, 0:H]), delta_t) + mm3((envN[l, 0], envN[l, 1]), padded2(d_u_t))
        dlat_t = dlat_t + back
    step(0, a_to_b)
    keep_d(2, 1, dlat_t * sp[0] + dlat[0] * (spp[0] * first_t))
    feats2 = split(jnp.concatenate([feats_t, feats], axis=1))
    out_sum = split(lat2_t * env + lat[2] * env_t)
    osum[0], osum[1] = out_sum
    ones = jnp.ones((16, E), BF16)

    def rest(h, slot):
        rows = pl.ds(pl.multiple_of(h * 256, 256), 256)
        h2[slot, 0:576] = gradient(0, h)
        for l in (1, 0):
            h2[slot, 640 - 64 * l : 704 - 64 * l] = mm3(env_rows[l], (xh[l, rows], xl[l, rows]), NT)
        h2[slot, 704:736] = mm3(feats2, (dh[2, rows], dl[2, rows]), NT)
        o = dot(ones, osum[0, rows], NT) + dot(ones, osum[1, rows], NT)
        h2[slot, 728:736] = o[0:8]
        h2[slot, 736:768] = jnp.zeros((32, 256), F32)

    rest(1 - core, 0)
    step(1, start_core)
    rest(core, 1)
    step(0, b_to_c)
    step(1, core_to_a)
    step(0, c_to_b)
    step(1, a_to_b)
    step(0, b_to_a)
    step(1, b_to_c)
    step(0, a_to_core)
    step(1, c_to_b)
    step(1, b_to_a)
    step(0, finish)
    step(1, a_to_core)
    step(1, finish)
    for c in sends:
        c.wait_send()


def unpack(g1_ref, g2_ref, rad_ref, cem_ref, nem_ref, env_ref, lat_ref, out_ref):
    lat_ref[1] = g1_ref[...]
    lat_ref[0] = g2_ref[0:576]
    env_ref[1] = g2_ref[576:640]
    env_ref[0] = g2_ref[640:704]
    rad_ref[...] = g2_ref[704:712]
    cem_ref[...] = g2_ref[712:717]
    nem_ref[...] = g2_ref[720:725]
    out_ref[...] = g2_ref[728:729]


def shape(*dims):
    return jax.ShapeDtypeStruct(dims, F32)


def on_device(
    positions, species, export_index, edge_center, edge_neighbor, edge_count, force_target, radial_weight, center_embed,
    neighbor_embed, environment_weight, latent_weight, output_weight,
):
    vmem = pl.BlockSpec(memory_space=VMEM)
    scratch = [
        VMEM((2, 576, 512), F32),
        VMEM((2, 64, 512), F32),
        VMEM((2, 2, 512, 640), BF16),
        VMEM((2, 2, 576, 512), BF16),
        VMEM((2, 2, 64, 512), BF16),
        VMEM((2, 2, 512, 128), BF16),
        VMEM((32, 512), F32),
        VMEM((H, E), F32),
        VMEM((10, 8, 128), F32),
        VMEM((10, 8, 128), F32),
        VMEM((2, 8, 128), F32),
        VMEM((9, 8, 128), F32),
        VMEM((9, 8, 128), F32),
        VMEM((3, H, E), F32),
        VMEM((2, 576, 512), BF16),
        VMEM((2, 576, 512), BF16),
        VMEM((3, 512, 512), BF16),
        VMEM((3, 512, 512), BF16),
        VMEM((3, H, E), F32),
        VMEM((3, H, E), F32),
        VMEM((3, H, E), F32),
        VMEM((2, H, E), BF16),
        VMEM((2, 3 * M, E), F32),
        VMEM((2, 3 * M, E), F32),
        VMEM((2, M, E), F32),
    ]
    for n in ROWS:
        scratch.append(VMEM((2, n, 256), F32))
    for n in ROWS:
        scratch.append(VMEM((n, 256), F32))
    for n in PARTS:
        scratch.append(VMEM((3, 3, n[0] // 4, 256), F32))
    for _ in range(2):
        for n in PARTS:
            scratch.append(VMEM((3, 3, n[0] // 8, 128), F32))
    scratch += [
        pltpu.SemaphoreType.DMA((2,)),
        pltpu.SemaphoreType.DMA((3, 8)),
        pltpu.SemaphoreType.DMA((3, 8)),
        pltpu.SemaphoreType.DMA((2, 3, 17)),
        pltpu.SemaphoreType.DMA((2, 3, 17)),
    ]
    any_space = pl.BlockSpec(memory_space=pl.ANY)
    forces, g1, g2 = pl.pallas_call(
        kernel,
        out_shape=(shape(3, 1, 1, ATOMS), shape(ROWS[0], 512), shape(ROWS[1], 512)),
        in_specs=[vmem] * 11 + [any_space] * 2,
        out_specs=(vmem,) * 3,
        scratch_shapes=scratch,
        compiler_params=pltpu.CompilerParams(collective_id=0, has_side_effects=True, vmem_limit_bytes=56 << 20),
        name="step",
    )(
        positions, species, export_index, edge_center, edge_neighbor, edge_count, force_target, radial_weight, center_embed,
        neighbor_embed, output_weight.reshape(1, 512), jnp.swapaxes(environment_weight, 1, 2), latent_weight,
    )
    grads = pl.pallas_call(
        unpack,
        out_shape=(shape(8, 512), shape(5, 512), shape(5, 512), shape(2, 64, 512), shape(2, 576, 512), shape(1, 512)),
        in_specs=[vmem] * 2,
        out_specs=(vmem,) * 6,
        compiler_params=pltpu.CompilerParams(vmem_limit_bytes=32 << 20),
        name="unpack",
    )(g1, g2)
    radial, near, far, environment, latent, output = grads
    return forces, radial, near, far, jnp.swapaxes(environment, 1, 2), latent, output.reshape(512)


def solution(mesh):
    return jax.shard_map(
        on_device,
        mesh=mesh,
        in_specs=(
            P(None, "slab", "brick", None),
            P("slab", "brick", None),
            P("slab", "brick", None),
            P("slab", "brick", None),
            P("slab", "brick", None),
            P("slab", "brick"),
            P(None, "slab", "brick", None),
            P(),
            P(),
            P(),
            P(),
            P(),
            P(),
        ),
        out_specs=(P(None, "slab", "brick", None), P(), P(), P(), P(), P(), P()),
        check_vma=False,
    )
```

time: 335 us -> 85.8 us (0.26)
  waiting for transfers between devices: 109 us -> 0 us
  Pallas kernels: 0 us -> 81.1 us
  blocking collectives: 65 us -> 0 us
  matrix products: 60.4 us -> 0 us
  starting transfers between devices: 37 us -> 0 us
  local copies, waits for them, and re-layouts: 26.1 us -> 3.24 us
  other arithmetic: 18.2 us -> 0 us
  between operations: 16.7 us -> 1.31 us
    pallas_call x0 -> x2, Pallas kernels: none -> 81.1 us  [the longest x1 79.4 us: on_device(): pl.pallas_call(kernel, out_shape=(shape(3, 1, 1, ATOMS), shape(ROWS[0], 5...]
    psum x1 -> x0, waiting for transfers between devices: 80.7 us -> none  [on_device(): grads = lax.psum(local, ('slab', 'brick'))]
    psum x1 -> x0, blocking collectives: 65 us -> none  [on_device(): grads = lax.psum(local, ('slab', 'brick'))]
    dot_general x82 -> x0, matrix products: 60.4 us -> none  [product(): jnp.dot(left, right, precision=lax.Precision.HIGHEST, preferred_element_t...]
    ppermute x20 -> x0, starting transfers between devices: 36.9 us -> none  [the longest x12 20.2 us: passed_along(): lax.ppermute(x, axis, [(i, (i + by) % devices) for i in range(devices)])]
    ppermute x20 -> x0, waiting for transfers between devices: 27.9 us -> none  [the longest x4 14.4 us: with_halo(): before = lax.ppermute(last, axis, up)]
    gather x14 -> x0, local copies, waits for them, and re-layouts: 10.4 us -> none  [the longest x8 5.69 us: edge_energy(): vectors = table_pos[:, neighbor] - table_pos[:, center]]
    unnamed x173 -> x7, local copies, waits for them, and re-layouts: 10.9 us -> 3.24 us
  transfers between devices with their start and end apart: 21 -> 0, of which waited for: 8 -> 0; matrix products, arithmetic and copies ran while one was open for 2% -> 0% of each run, Pallas kernels for 0% -> 0%
where the time goes in v1:
time: 85.8 us; the launch traced here: 85.6 us
  Pallas kernels  81.1 us (95%)
  local copies, waits for them, and re-layouts  3.24 us (4%)
  between operations  1.31 us (2%)
    pallas_call x1, Pallas kernels, on_device(): pl.pallas_call(kernel, out_shape=(shape(3, 1, 1, ATOMS), shape(ROWS[0], 5...  79.4 us
    unnamed x7, local copies, waits for them, and re-layouts  3.24 us

profile of v1, /device:TPU:1, one launch (start us, length us, event | category | flops | bytes accessed | tf_op | source)
XLA Modules:
  0.0 85.6 jit_solution(13879123485024243522)
XLA Ops:
  1.3 79.4 %step.1 = (f32[3,1,1,128]{3,2,1,0:T(1,128)}, f32[576,512]{1,0:T(8,128)}, f32[768,512]{1,0:T(8,128)}) custom-call(f32[3,1,1,128]{3,2,1,0:T(1,128)} %pos_ref.1, s32[1,1,128]{2,1,0:T(1,128)} %spec_ref.1, s32[1,1,128]{2,1,0:T(1,128)} %exp_ref.1, s32[1,1,256]{2,1,0:T(1,128)} %cen_ref.1, s32[1,1,256]{2,1,0:T(1,128)} %nbr_ref.1, s32[1,1]{1,0:T(1,128)S(6)} %copy.21.cnt_ref, ...), custom_call_target="tpu_custom_call" | custom-call | tf_op jit(solution)/shard_map/step/pallas_call | solution.py:545
  80.7 0.0 copy-start.2
  80.7 0.0 copy-start
  80.7 1.4 %copy-done = f32[768,512]{1,0:T(8,128)S(1)} copy-done((f32[768,512]{1,0:T(8,128)S(1)}, f32[768,512]{1,0:T(8,128)}, u32[]{:S(2)}) %copy-start) | copy-done | bytes 1572888
  82.1 0.0 copy-start.1
  82.1 1.3 %copy-done.1 = f32[576,512]{1,0:T(8,128)S(1)} copy-done((f32[576,512]{1,0:T(8,128)S(1)}, f32[576,512]{1,0:T(8,128)}, u32[]{:S(2)}) %copy-start.1) | copy-done | bytes 1179672
  83.4 1.7 %unpack.1 = (f32[8,512]{1,0:T(8,128)}, f32[5,512]{1,0:T(8,128)}, f32[5,512]{1,0:T(8,128)}, f32[2,64,512]{2,1,0:T(8,128)}, f32[2,576,512]{2,1,0:T(8,128)}, /*index=5*/f32[1,512]{1,0:T(1,128)}) custom-call(f32[576,512]{1,0:T(8,128)S(1)} %copy-done.1, f32[768,512]{1,0:T(8,128)S(1)} %copy-done), custom_call_target="tpu_custom_call" | custom-call | tf_op jit(solution)/shard_map/unpack/pallas_call | solution.py:557
  85.0 0.0 copy-done.2
  85.0 0.6 copy.22
Async XLA Ops:
  80.7 4.4 %copy-start.2 = (f32[3,1,1,128]{3,2,1,0:T(1,128)S(1)}, f32[3,1,1,128]{3,2,1,0:T(1,128)}, u32[]{:S(2)}) copy-start(f32[3,1,1,128]{3,2,1,0:T(1,128)} %get-tuple-element.32) | copy-start | bytes 4612
  80.7 1.4 %copy-start = (f32[768,512]{1,0:T(8,128)S(1)}, f32[768,512]{1,0:T(8,128)}, u32[]{:S(2)}) copy-start(f32[768,512]{1,0:T(8,128)} %get-tuple-element.18.g2_ref) | copy-start | bytes 4718596
  82.1 1.3 %copy-start.1 = (f32[576,512]{1,0:T(8,128)S(1)}, f32[576,512]{1,0:T(8,128)}, u32[]{:S(2)}) copy-start(f32[576,512]{1,0:T(8,128)} %get-tuple-element.17.g1_ref) | copy-start | bytes 3538948

commit v2 on v1

--- a/solution.py
+++ b/solution.py
@@ -21,8 +21,8 @@
 
 N_SLAB, N_BRICK = 4, 32
 H, M, E, ATOMS = 512, 64, 256, 128
-ROWS = (576, 768)
-PARTS = ((192, 192, 192), (256, 256, 256))
+ROWS = (576, 576, 192)
+PARTS = tuple((n // 3,) * 3 for n in ROWS)
 ORDERS = (("x", "y", "z"), ("y", "z", "x"), ("z", "x", "y"))
 NEIGHBOURS = [(p, q) for p in range(3) for q in range(3) if (p, q) != (1, 1)]
 
@@ -79,11 +79,11 @@
 
 def kernel(
     pos_ref, spec_ref, exp_ref, cen_ref, nbr_ref, cnt_ref, tgt_ref, rad_ref, cem_ref, nem_ref, ow_ref, env_hbm, lat_hbm,
-    forces_ref, g1_ref, g2_ref,
+    forces_ref, g1_ref, g2_ref, g3_ref,
     w_lat, w_env, latT, latN, envT, envN, a0, oc,
     tbl, ttbl, sendbuf, gsend, grecv,
     lat, xh, xl, dh, dl, sp, spp, dlat, osum, tt, pp, uu,
-    h1, h2, c1, c2, ra1, ra2, rb1, rb2, rc1, rc2,
+    h1, h2, h3, c1, c2, c3, ra1, ra2, ra3, rb1, rb2, rb3, rc1, rc2, rc3,
     wsem, hs, hr, ars, arr,
 ):
     s, b = lax.axis_index("slab"), lax.axis_index("brick")
@@ -199,8 +199,13 @@
     def activation(i, value):
         g = sigmoid(value)
         sp[i] = g * (1.0 + value * (1.0 - g))
+        spp[i] = value
+        return value * g
+
+    def second_derivative(i):
+        value = spp[i]
+        g = sigmoid(value)
         spp[i] = (g * (1.0 - g)) * (2.0 + value * (1.0 - 2.0 * g))
-        return value * g
 
     def keep_x(l, half, rows, value):
         high, low = split(value)
@@ -273,6 +278,8 @@
         gsend[k] = d_table[:, ATOMS * (k + 1) : ATOMS * (k + 2)]
     second = halo(1, lambda k: gsend.at[k], lambda k: grecv.at[k], True)
     sends += second
+    second_derivative(0)
+    second_derivative(1)
     for c in second:
         c.wait_recv()
     returned = gsend[4]
@@ -288,6 +295,7 @@
     third = halo(2, lambda k: sendbuf.at[1], lambda k: ttbl.at[1 + k], False)
     sends += third
     ttbl[5] = sendbuf[1]
+    second_derivative(2)
     vc = select(ttbl[0], hot_c)
     for c in third:
         c.wait_recv()
@@ -315,10 +323,10 @@
         update_t[l] = mm3((latT[l, 0, :, 0:H], latT[l, 1, :, 0:H]), now) + mm3((latT[l, 0, :, H:], latT[l, 1, :, H:]), padded2(inv_t))
         lat_t = lat_t + sp[l + 1] * update_t[l]
 
-    half = (h1, h2)
-    from_core = (c1, c2)
-    from_a, from_b, from_c = (ra1, ra2), (rb1, rb2), (rc1, rc2)
-    result = (g1_ref, g2_ref)
+    half = (h1, h2, h3)
+    from_core = (c1, c2, c3)
+    from_a, from_b, from_c = (ra1, ra2, ra3), (rb1, rb2, rb3), (rc1, rc2, rc3)
+    result = (g1_ref, g2_ref, g3_ref)
     flying = {}
 
     def place(g, i):
@@ -347,18 +355,25 @@
     def lanes_at(first, count=128):
         return pl.ds(pl.multiple_of(first, 128), count)
 
-    def start_core(g, i):
-        n, row0, *_ = place(g, i)
-        copy(g, i, 0, half[g].at[0, row0 : row0 + n], from_core[g].at[row0 : row0 + n], partner)
-
-    def core_to_a(g, i):
+    def chunk(g, i, k):
         n, row0, a, *_ = place(g, i)
-        lands(g, i, 0)
-        rows = slice(row0, row0 + n)
-        half[g][1, rows] = half[g][1, rows] + from_core[g][rows]
-        for k in (1, 2, 3):
-            theirs = row0 + lax.rem(at[a] + k, 4) * (n // 4)
-            copy(g, i, k, half[g].at[1, pl.ds(pl.multiple_of(theirs, 8), n // 4)], from_a[g].at[i, k - 1], peer(a, k))
+        return pl.ds(pl.multiple_of(row0 + lax.rem(at[a] + k, 4) * (n // 4), 8), n // 4)
+
+    def start_core(g):
+        for k in (2, 1, 3, 0):
+            for i in range(3):
+                rows = chunk(g, i, k)
+                copy(g, i, 16 + k, half[g].at[0, rows], from_core[g].at[rows], partner)
+
+    def core_to_a(g):
+        for k in (2, 1, 3, 0):
+            for i in range(3):
+                lands(g, i, 16 + k)
+                rows = chunk(g, i, k)
+                half[g][1, rows] = half[g][1, rows] + from_core[g][rows]
+                if k:
+                    a = ORDERS[i][0]
+                    copy(g, i, k, half[g].at[1, rows], from_a[g].at[i, k - 1], peer(a, k))
 
     def a_to_b(g, i):
         n, row0, a, bb, c, row_a, row_b = place(g, i)
@@ -397,18 +412,21 @@
         for k in (1, 2, 3):
             lands(g, i, 9 + k)
         here = result[g].at[pl.ds(row_a, n // 4), lanes_at(core * 256, 256)]
-        for k in (1, 2, 3):
+        for k in (2, 1, 3):
             copy(g, i, 12 + k, here, here, peer(a, k))
-
-    def a_to_core(g, i):
-        n, row0, *_ = place(g, i)
-        for k in (1, 2, 3):
-            lands(g, i, 12 + k)
-        here = result[g].at[row0 : row0 + n, lanes_at(core * 256, 256)]
-        copy(g, i, 16, here, here, partner)
-
-    def finish(g, i):
-        lands(g, i, 16)
+        copy(g, i, 20, here, here, partner)
+
+    def a_to_core(g):
+        for k in (1, 3, 2):
+            for i in range(3):
+                lands(g, i, 12 + k)
+                here = result[g].at[chunk(g, i, 4 - k), lanes_at(core * 256, 256)]
+                copy(g, i, 20 + k, here, here, partner)
+
+    def finish(g):
+        for i in range(3):
+            for k in range(4):
+                lands(g, i, 20 + k)
 
     def step(g, f):
         for i in range(3):
@@ -422,7 +440,7 @@
     scaled = oc[...] * env_t
     delta_t = keep_d(1, 1, scaled * sp[2] + dlat[2] * (spp[2] * update_t[1]))
     h1[0] = gradient(1, 1 - core)
-    step(0, start_core)
+    start_core(0)
     h1[1] = gradient(1, core)
 
     dlat_t = scaled
@@ -430,7 +448,10 @@
     for l in (1, 0):
         if l == 0:
             delta_t = keep_d(0, 1, dlat_t * sp[1] + dlat[1] * (spp[1] * update_t[0]))
-            step(0, core_to_a)
+            core_to_a(0)
+            h2[0] = gradient(0, 1 - core)
+            start_core(1)
+            h2[1] = gradient(0, core)
         d_inv_t = mm3((latN[l, 0, H:], latN[l, 1, H:]), delta_t)
         d_inv3, d_t, d_w, d_u = kept[l]
         t_t, pr_t = kept_t[l]
@@ -442,7 +463,7 @@
         env_rows[l] = (jnp.concatenate([d_u[0], d_u_t[0]], axis=1), jnp.concatenate([d_u[1], d_u_t[1]], axis=1))
         back = mm3((latN[l, 0, 0:H], latN[l, 1, 0:H]), delta_t) + mm3((envN[l, 0], envN[l, 1]), padded2(d_u_t))
         dlat_t = dlat_t + back
-    step(0, a_to_b)
+    core_to_a(1)
     keep_d(2, 1, dlat_t * sp[0] + dlat[0] * (spp[0] * first_t))
     feats2 = split(jnp.concatenate([feats_t, feats], axis=1))
     out_sum = split(lat2_t * env + lat[2] * env_t)
@@ -451,42 +472,48 @@
 
     def rest(h, slot):
         rows = pl.ds(pl.multiple_of(h * 256, 256), 256)
-        h2[slot, 0:576] = gradient(0, h)
         for l in (1, 0):
-            h2[slot, 640 - 64 * l : 704 - 64 * l] = mm3(env_rows[l], (xh[l, rows], xl[l, rows]), NT)
-        h2[slot, 704:736] = mm3(feats2, (dh[2, rows], dl[2, rows]), NT)
+            h3[slot, 64 - 64 * l : 128 - 64 * l] = mm3(env_rows[l], (xh[l, rows], xl[l, rows]), NT)
+        h3[slot, 128:160] = mm3(feats2, (dh[2, rows], dl[2, rows]), NT)
         o = dot(ones, osum[0, rows], NT) + dot(ones, osum[1, rows], NT)
-        h2[slot, 728:736] = o[0:8]
-        h2[slot, 736:768] = jnp.zeros((32, 256), F32)
+        h3[slot, 152:160] = o[0:8]
+        h3[slot, 160:192] = jnp.zeros((32, 256), F32)
 
     rest(1 - core, 0)
-    step(1, start_core)
+    start_core(2)
     rest(core, 1)
+    step(0, a_to_b)
+    core_to_a(2)
     step(0, b_to_c)
-    step(1, core_to_a)
+    step(1, a_to_b)
+    step(2, a_to_b)
     step(0, c_to_b)
-    step(1, a_to_b)
+    step(1, b_to_c)
+    step(2, b_to_c)
     step(0, b_to_a)
-    step(1, b_to_c)
-    step(0, a_to_core)
     step(1, c_to_b)
+    step(2, c_to_b)
     step(1, b_to_a)
-    step(0, finish)
-    step(1, a_to_core)
-    step(1, finish)
+    a_to_core(0)
+    step(2, b_to_a)
+    a_to_core(1)
+    a_to_core(2)
+    for g in range(3):
+        finish(g)
     for c in sends:
         c.wait_send()
 
 
-def unpack(g1_ref, g2_ref, rad_ref, cem_ref, nem_ref, env_ref, lat_ref, out_ref):
+def unpack(f_ref, g1_ref, g2_ref, g3_ref, forces_ref, rad_ref, cem_ref, nem_ref, env_ref, lat_ref, out_ref):
     lat_ref[1] = g1_ref[...]
-    lat_ref[0] = g2_ref[0:576]
-    env_ref[1] = g2_ref[576:640]
-    env_ref[0] = g2_ref[640:704]
-    rad_ref[...] = g2_ref[704:712]
-    cem_ref[...] = g2_ref[712:717]
-    nem_ref[...] = g2_ref[720:725]
-    out_ref[...] = g2_ref[728:729]
+    lat_ref[0] = g2_ref[...]
+    env_ref[1] = g3_ref[0:64]
+    env_ref[0] = g3_ref[64:128]
+    rad_ref[...] = g3_ref[128:136]
+    cem_ref[...] = g3_ref[136:141]
+    nem_ref[...] = g3_ref[144:149]
+    out_ref[...] = g3_ref[152:153]
+    forces_ref[...] = f_ref[...]
 
 
 def shape(*dims):
@@ -531,22 +558,22 @@
         scratch.append(VMEM((n, 256), F32))
     for n in PARTS:
         scratch.append(VMEM((3, 3, n[0] // 4, 256), F32))
-    for _ in range(2):
+    for _ in (1, 2):
         for n in PARTS:
             scratch.append(VMEM((3, 3, n[0] // 8, 128), F32))
     scratch += [
         pltpu.SemaphoreType.DMA((2,)),
         pltpu.SemaphoreType.DMA((3, 8)),
         pltpu.SemaphoreType.DMA((3, 8)),
-        pltpu.SemaphoreType.DMA((2, 3, 17)),
-        pltpu.SemaphoreType.DMA((2, 3, 17)),
+        pltpu.SemaphoreType.DMA((3, 3, 24)),
+        pltpu.SemaphoreType.DMA((3, 3, 24)),
     ]
     any_space = pl.BlockSpec(memory_space=pl.ANY)
-    forces, g1, g2 = pl.pallas_call(
+    parts = pl.pallas_call(
         kernel,
-        out_shape=(shape(3, 1, 1, ATOMS), shape(ROWS[0], 512), shape(ROWS[1], 512)),
+        out_shape=(VMEM((3, 1, 1, ATOMS), F32),) + tuple(VMEM((n, 512), F32) for n in ROWS),
         in_specs=[vmem] * 11 + [any_space] * 2,
-        out_specs=(vmem,) * 3,
+        out_specs=(vmem,) * 4,
         scratch_shapes=scratch,
         compiler_params=pltpu.CompilerParams(collective_id=0, has_side_effects=True, vmem_limit_bytes=56 << 20),
         name="step",
@@ -554,15 +581,15 @@
         positions, species, export_index, edge_center, edge_neighbor, edge_count, force_target, radial_weight, center_embed,
         neighbor_embed, output_weight.reshape(1, 512), jnp.swapaxes(environment_weight, 1, 2), latent_weight,
     )
-    grads = pl.pallas_call(
+    outs = pl.pallas_call(
         unpack,
-        out_shape=(shape(8, 512), shape(5, 512), shape(5, 512), shape(2, 64, 512), shape(2, 576, 512), shape(1, 512)),
-        in_specs=[vmem] * 2,
-        out_specs=(vmem,) * 6,
+        out_shape=(shape(3, 1, 1, ATOMS), shape(8, 512), shape(5, 512), shape(5, 512), shape(2, 64, 512), shape(2, 576, 512), shape(1, 512)),
+        in_specs=[vmem] * 4,
+        out_specs=(vmem,) * 7,
         compiler_params=pltpu.CompilerParams(vmem_limit_bytes=32 << 20),
         name="unpack",
-    )(g1, g2)
-    radial, near, far, environment, latent, output = grads
+    )(*parts)
+    forces, radial, near, far, environment, latent, output = outs
     return forces, radial, near, far, jnp.swapaxes(environment, 1, 2), latent, output.reshape(512)
 
 

time: 85.8 us -> 78.1 us (0.910)
  Pallas kernels: 81.1 us -> 76.6 us
  local copies, waits for them, and re-layouts: 3.24 us -> 0 us
    pallas_call x2, Pallas kernels: 81.1 us -> 76.6 us  [the longest x1 74.9 us: on_device(): pl.pallas_call(kernel, out_shape=(VMEM((3, 1, 1, ATOMS), F32),) + tuple((...]
    unnamed x7 -> x0, local copies, waits for them, and re-layouts: 3.24 us -> none
where the time goes in v2:
time: 78.1 us; the launch traced here: 77.9 us
  Pallas kernels  76.6 us (98%)
  between operations  1.29 us (2%)
    pallas_call x1, Pallas kernels, on_device(): pl.pallas_call(kernel, out_shape=(VMEM((3, 1, 1, ATOMS), F32),) + tuple((...  74.9 us
    pallas_call x1, Pallas kernels, on_device(): pl.pallas_call(unpack, out_shape=(shape(3, 1, 1, ATOMS), shape(8, 512), s...  1.67 us

profile of v2, /device:TPU:1, one launch (start us, length us, event | category | flops | bytes accessed | tf_op | source)
XLA Modules:
  0.0 77.9 jit_solution(2143718894332874055)
XLA Ops:
  1.3 74.9 %step.1 = (f32[3,1,1,128]{3,2,1,0:T(1,128)S(1)}, f32[576,512]{1,0:T(8,128)S(1)}, f32[576,512]{1,0:T(8,128)S(1)}, f32[192,512]{1,0:T(8,128)S(1)}) custom-call(f32[3,1,1,128]{3,2,1,0:T(1,128)} %pos_ref.1, s32[1,1,128]{2,1,0:T(1,128)} %spec_ref.1, s32[1,1,128]{2,1,0:T(1,128)} %exp_ref.1, s32[1,1,256]{2,1,0:T(1,128)} %cen_ref.1, s32[1,1,256]{2,1,0:T(1,128)} %nbr_ref.1, ...), custom_call_target="tpu_custom_call" | custom-call | tf_op jit(solution)/shard_map/step/pallas_call | solution.py:572
  76.2 1.7 %unpack.1 = (f32[3,1,1,128]{3,2,1,0:T(1,128)}, f32[8,512]{1,0:T(8,128)}, f32[5,512]{1,0:T(8,128)}, f32[5,512]{1,0:T(8,128)}, f32[2,64,512]{2,1,0:T(8,128)}, /*index=5*/f32[2,576,512]{2,1,0:T(8,128)}, f32[1,512]{1,0:T(1,128)}) custom-call(f32[3,1,1,128]{3,2,1,0:T(1,128)S(1)} %get-tuple-element.18.f_ref, f32[576,512]{1,0:T(8,128)S(1)} %get-tuple-element.19.g1_ref, ...), custom_call_target="tpu_custom_call" | custom-call | tf_op jit(solution)/shard_map/unpack/pallas_call | solution.py:584

commit v3 on v2

--- a/solution.py
+++ b/solution.py
@@ -24,7 +24,7 @@
 ROWS = (576, 576, 192)
 PARTS = tuple((n // 3,) * 3 for n in ROWS)
 ORDERS = (("x", "y", "z"), ("y", "z", "x"), ("z", "x", "y"))
-NEIGHBOURS = [(p, q) for p in range(3) for q in range(3) if (p, q) != (1, 1)]
+NEIGHBOURS = [(p, q) for q in (0, 2, 1) for p in (0, 2, 1) if (p, q) != (1, 1)]
 
 
 def dot(a, b, dims=NN):
@@ -327,7 +327,7 @@
     from_core = (c1, c2, c3)
     from_a, from_b, from_c = (ra1, ra2, ra3), (rb1, rb2, rb3), (rc1, rc2, rc3)
     result = (g1_ref, g2_ref, g3_ref)
-    flying = {}
+    flying, done = {}, []
 
     def place(g, i):
         n = PARTS[g][i]
@@ -427,6 +427,42 @@
         for i in range(3):
             for k in range(4):
                 lands(g, i, 20 + k)
+
+    def whole_chunk(g, i):
+        row_a = place(g, i)[5]
+        return half[g].at[1, pl.ds(row_a, PARTS[g][i] // 4)]
+
+    def exchange(g, i, first, came_from, axis):
+        here = whole_chunk(g, i)
+        for k in (2, 1, 3):
+            copy(g, i, first + k, here, came_from[g].at[i, k - 1], peer(axis, k))
+
+    def a_to_b_whole(g, i):
+        for k in (1, 2, 3):
+            lands(g, i, k)
+        here = whole_chunk(g, i)
+        here[...] = (here[...] + from_a[g][i, 1]) + (from_a[g][i, 0] + from_a[g][i, 2])
+        exchange(g, i, 3, from_b, ORDERS[i][1])
+
+    def b_to_c_whole(g, i):
+        for k in (1, 2, 3):
+            lands(g, i, 3 + k)
+            flying[g, i, 3 + k].wait_send()
+            done.append(flying[g, i, 3 + k])
+        here = whole_chunk(g, i)
+        here[...] = (here[...] + from_b[g][i, 1]) + (from_b[g][i, 0] + from_b[g][i, 2])
+        exchange(g, i, 6, from_c, ORDERS[i][2])
+
+    def c_to_a_whole(g, i):
+        for k in (1, 2, 3):
+            lands(g, i, 6 + k)
+        n, row0, a, bb, c, row_a, row_b = place(g, i)
+        out = result[g].at[pl.ds(row_a, n // 4), lanes_at(core * 256, 256)]
+        here = whole_chunk(g, i)
+        out[...] = (here[...] + from_c[g][i, 1]) + (from_c[g][i, 0] + from_c[g][i, 2])
+        for k in (2, 1, 3):
+            copy(g, i, 12 + k, out, out, peer(a, k))
+        copy(g, i, 20, out, out, partner)
 
     def step(g, f):
         for i in range(3):
@@ -484,24 +520,24 @@
     rest(core, 1)
     step(0, a_to_b)
     core_to_a(2)
+    step(1, a_to_b)
     step(0, b_to_c)
-    step(1, a_to_b)
-    step(2, a_to_b)
+    step(2, a_to_b_whole)
+    step(1, b_to_c)
     step(0, c_to_b)
-    step(1, b_to_c)
-    step(2, b_to_c)
+    step(2, b_to_c_whole)
+    step(1, c_to_b)
     step(0, b_to_a)
-    step(1, c_to_b)
-    step(2, c_to_b)
+    step(2, c_to_a_whole)
     step(1, b_to_a)
     a_to_core(0)
-    step(2, b_to_a)
+    a_to_core(2)
     a_to_core(1)
-    a_to_core(2)
     for g in range(3):
         finish(g)
     for c in sends:
-        c.wait_send()
+        if not any(c is d for d in done):
+            c.wait_send()
 
 
 def unpack(f_ref, g1_ref, g2_ref, g3_ref, forces_ref, rad_ref, cem_ref, nem_ref, env_ref, lat_ref, out_ref):
@@ -559,8 +595,9 @@
     for n in PARTS:
         scratch.append(VMEM((3, 3, n[0] // 4, 256), F32))
     for _ in (1, 2):
-        for n in PARTS:
+        for n in PARTS[:2]:
             scratch.append(VMEM((3, 3, n[0] // 8, 128), F32))
+        scratch.append(VMEM((3, 3, PARTS[2][0] // 4, 256), F32))
     scratch += [
         pltpu.SemaphoreType.DMA((2,)),
         pltpu.SemaphoreType.DMA((3, 8)),

time: 78.1 us -> 74.2 us (0.950)
  Pallas kernels: 76.6 us -> 72.7 us
    pallas_call x1, Pallas kernels: 74.9 us -> 71 us  [on_device(): pl.pallas_call(kernel, out_shape=(VMEM((3, 1, 1, ATOMS), F32),) + tuple((...]
where the time goes in v3:
time: 74.2 us; the launch traced here: 74 us
  Pallas kernels  72.7 us (98%)
  between operations  1.29 us (2%)
    pallas_call x1, Pallas kernels, on_device(): pl.pallas_call(kernel, out_shape=(VMEM((3, 1, 1, ATOMS), F32),) + tuple((...  71 us
    pallas_call x1, Pallas kernels, on_device(): pl.pallas_call(unpack, out_shape=(shape(3, 1, 1, ATOMS), shape(8, 512), s...  1.67 us

profile of v3, /device:TPU:1, one launch (start us, length us, event | category | flops | bytes accessed | tf_op | source)
XLA Modules:
  0.0 74.0 jit_solution(167535233002041324)
XLA Ops:
  1.3 71.0 %step.1 = (f32[3,1,1,128]{3,2,1,0:T(1,128)S(1)}, f32[576,512]{1,0:T(8,128)S(1)}, f32[576,512]{1,0:T(8,128)S(1)}, f32[192,512]{1,0:T(8,128)S(1)}) custom-call(f32[3,1,1,128]{3,2,1,0:T(1,128)} %pos_ref.1, s32[1,1,128]{2,1,0:T(1,128)} %spec_ref.1, s32[1,1,128]{2,1,0:T(1,128)} %exp_ref.1, s32[1,1,256]{2,1,0:T(1,128)} %cen_ref.1, s32[1,1,256]{2,1,0:T(1,128)} %nbr_ref.1, ...), custom_call_target="tpu_custom_call" | custom-call | tf_op jit(solution)/shard_map/step/pallas_call | solution.py:609
  72.3 1.7 %unpack.1 = (f32[3,1,1,128]{3,2,1,0:T(1,128)}, f32[8,512]{1,0:T(8,128)}, f32[5,512]{1,0:T(8,128)}, f32[5,512]{1,0:T(8,128)}, f32[2,64,512]{2,1,0:T(8,128)}, /*index=5*/f32[2,576,512]{2,1,0:T(8,128)}, f32[1,512]{1,0:T(1,128)}) custom-call(f32[3,1,1,128]{3,2,1,0:T(1,128)S(1)} %get-tuple-element.18.f_ref, f32[576,512]{1,0:T(8,128)S(1)} %get-tuple-element.19.g1_ref, ...), custom_call_target="tpu_custom_call" | custom-call | tf_op jit(solution)/shard_map/unpack/pallas_call | solution.py:621

commit v4 on v3

--- a/solution.py
+++ b/solution.py
@@ -78,8 +78,9 @@
 
 
 def kernel(
-    pos_ref, spec_ref, exp_ref, cen_ref, nbr_ref, cnt_ref, tgt_ref, rad_ref, cem_ref, nem_ref, ow_ref, env_hbm, lat_hbm,
+    pos_in, spec_in, exp_in, cen_in, nbr_in, cnt_ref, tgt_in, rad_in, cem_in, nem_in, ow_in, env_hbm, lat_hbm,
     forces_ref, g1_ref, g2_ref, g3_ref,
+    pos_ref, spec_ref, exp_ref, cen_ref, nbr_ref, tgt_ref, rad_ref, cem_ref, nem_ref, ow_ref,
     w_lat, w_env, latT, latN, envT, envN, a0, oc,
     tbl, ttbl, sendbuf, gsend, grecv,
     lat, xh, xl, dh, dl, sp, spp, dlat, osum, tt, pp, uu,
@@ -109,8 +110,24 @@
         pltpu.make_async_copy(env_hbm, w_env, wsem.at[0]),
         pltpu.make_async_copy(lat_hbm, w_lat, wsem.at[1]),
     ]
-    for c in loads:
+    firsts = [
+        pltpu.make_async_copy(pos_in, pos_ref, wsem.at[2]),
+        pltpu.make_async_copy(spec_in, spec_ref, wsem.at[3]),
+        pltpu.make_async_copy(exp_in, exp_ref, wsem.at[4]),
+    ]
+    loads += [
+        pltpu.make_async_copy(cen_in, cen_ref, wsem.at[5]),
+        pltpu.make_async_copy(nbr_in, nbr_ref, wsem.at[6]),
+        pltpu.make_async_copy(tgt_in, tgt_ref, wsem.at[7]),
+        pltpu.make_async_copy(rad_in, rad_ref, wsem.at[8]),
+        pltpu.make_async_copy(cem_in, cem_ref, wsem.at[9]),
+        pltpu.make_async_copy(nem_in, nem_ref, wsem.at[10]),
+        pltpu.make_async_copy(ow_in, ow_ref, wsem.at[11]),
+    ]
+    for c in firsts + loads:
         c.start()
+    for c in firsts:
+        c.wait()
 
     tbl[0] = jnp.zeros((8, ATOMS), F32)
     for m in range(3):
@@ -141,6 +158,8 @@
     sends += first
 
     tbl[5] = sendbuf[0]
+    for c in loads:
+        c.wait()
     center = cen_ref[0]
     hot_c = onehot(center, ATOMS)
     hot_n = onehot(nbr_ref[0], 10 * ATOMS)
@@ -154,8 +173,6 @@
     a0[8:13] = cem_ref[...]
     a0[16:21] = nem_ref[...]
     a0s = split(a0[...])
-    for c in loads:
-        c.wait()
     for l in range(2):
         w = w_lat[l]
         latN[l, 0], latN[l, 1] = split(w)
@@ -520,19 +537,18 @@
     rest(core, 1)
     step(0, a_to_b)
     core_to_a(2)
-    step(1, a_to_b)
+    step(1, a_to_b_whole)
     step(0, b_to_c)
     step(2, a_to_b_whole)
-    step(1, b_to_c)
+    step(1, b_to_c_whole)
     step(0, c_to_b)
     step(2, b_to_c_whole)
-    step(1, c_to_b)
+    step(1, c_to_a_whole)
     step(0, b_to_a)
     step(2, c_to_a_whole)
-    step(1, b_to_a)
+    a_to_core(1)
     a_to_core(0)
     a_to_core(2)
-    a_to_core(1)
     for g in range(3):
         finish(g)
     for c in sends:
@@ -562,6 +578,16 @@
 ):
     vmem = pl.BlockSpec(memory_space=VMEM)
     scratch = [
+        VMEM((3, 1, 1, ATOMS), F32),
+        VMEM((1, 1, ATOMS), jnp.int32),
+        VMEM((1, 1, ATOMS), jnp.int32),
+        VMEM((1, 1, E), jnp.int32),
+        VMEM((1, 1, E), jnp.int32),
+        VMEM((3, 1, 1, ATOMS), F32),
+        VMEM((8, H), F32),
+        VMEM((5, H), F32),
+        VMEM((5, H), F32),
+        VMEM((1, H), F32),
         VMEM((2, 576, 512), F32),
         VMEM((2, 64, 512), F32),
         VMEM((2, 2, 512, 640), BF16),
@@ -595,11 +621,10 @@
     for n in PARTS:
         scratch.append(VMEM((3, 3, n[0] // 4, 256), F32))
     for _ in (1, 2):
-        for n in PARTS[:2]:
-            scratch.append(VMEM((3, 3, n[0] // 8, 128), F32))
-        scratch.append(VMEM((3, 3, PARTS[2][0] // 4, 256), F32))
+        for g, n in enumerate(PARTS):
+            scratch.append(VMEM((3, 3) + ((n[0] // 4, 256) if g in (1, 2) else (n[0] // 8, 128)), F32))
     scratch += [
-        pltpu.SemaphoreType.DMA((2,)),
+        pltpu.SemaphoreType.DMA((12,)),
         pltpu.SemaphoreType.DMA((3, 8)),
         pltpu.SemaphoreType.DMA((3, 8)),
         pltpu.SemaphoreType.DMA((3, 3, 24)),
@@ -609,7 +634,7 @@
     parts = pl.pallas_call(
         kernel,
         out_shape=(VMEM((3, 1, 1, ATOMS), F32),) + tuple(VMEM((n, 512), F32) for n in ROWS),
-        in_specs=[vmem] * 11 + [any_space] * 2,
+        in_specs=[any_space] * 5 + [vmem] + [any_space] * 7,
         out_specs=(vmem,) * 4,
         scratch_shapes=scratch,
         compiler_params=pltpu.CompilerParams(collective_id=0, has_side_effects=True, vmem_limit_bytes=56 << 20),

time: 74.2 us -> 73 us (0.984)
  Pallas kernels: 72.7 us -> 71.6 us
    pallas_call x1, Pallas kernels: 71 us -> 69.9 us  [on_device(): pl.pallas_call(kernel, out_shape=(VMEM((3, 1, 1, ATOMS), F32),) + tuple((...]
where the time goes in v4:
time: 73 us; the launch traced here: 72.8 us
  Pallas kernels  71.6 us (98%)
  between operations  1.29 us (2%)
    pallas_call x1, Pallas kernels, on_device(): pl.pallas_call(kernel, out_shape=(VMEM((3, 1, 1, ATOMS), F32),) + tuple((...  69.9 us
    pallas_call x1, Pallas kernels, on_device(): pl.pallas_call(unpack, out_shape=(shape(3, 1, 1, ATOMS), shape(8, 512), s...  1.67 us

profile of v4, /device:TPU:1, one launch (start us, length us, event | category | flops | bytes accessed | tf_op | source)
XLA Modules:
  0.0 72.8 jit_solution(15566019785548254302)
XLA Ops:
  1.3 69.9 %step.1 = (f32[3,1,1,128]{3,2,1,0:T(1,128)S(1)}, f32[576,512]{1,0:T(8,128)S(1)}, f32[576,512]{1,0:T(8,128)S(1)}, f32[192,512]{1,0:T(8,128)S(1)}) custom-call(f32[3,1,1,128]{3,2,1,0:T(1,128)} %pos_in.1, s32[1,1,128]{2,1,0:T(1,128)} %spec_in.1, s32[1,1,128]{2,1,0:T(1,128)} %exp_in.1, s32[1,1,256]{2,1,0:T(1,128)} %cen_in.1, s32[1,1,256]{2,1,0:T(1,128)} %nbr_in.1, ...), custom_call_target="tpu_custom_call" | custom-call | tf_op jit(solution)/shard_map/step/pallas_call | solution.py:634
  71.2 1.7 %unpack.1 = (f32[3,1,1,128]{3,2,1,0:T(1,128)}, f32[8,512]{1,0:T(8,128)}, f32[5,512]{1,0:T(8,128)}, f32[5,512]{1,0:T(8,128)}, f32[2,64,512]{2,1,0:T(8,128)}, /*index=5*/f32[2,576,512]{2,1,0:T(8,128)}, f32[1,512]{1,0:T(1,128)}) custom-call(f32[3,1,1,128]{3,2,1,0:T(1,128)S(1)} %get-tuple-element.18.f_ref, f32[576,512]{1,0:T(8,128)S(1)} %get-tuple-element.19.g1_ref, ...), custom_call_target="tpu_custom_call" | custom-call | tf_op jit(solution)/shard_map/unpack/pallas_call | solution.py:646

commit v5 on v4

--- a/solution.py
+++ b/solution.py
@@ -70,7 +70,7 @@
 
 
 def sigmoid(x):
-    return 1.0 / (1.0 + jnp.exp(-x))
+    return 0.5 + 0.5 * jnp.tanh(0.5 * x)
 
 
 def device_at(core, x, y, z):
@@ -543,9 +543,14 @@
     step(1, b_to_c_whole)
     step(0, c_to_b)
     step(2, b_to_c_whole)
+    settled = len(sends)
     step(1, c_to_a_whole)
     step(0, b_to_a)
     step(2, c_to_a_whole)
+    for c in sends[:settled]:
+        if not any(c is d for d in done):
+            c.wait_send()
+            done.append(c)
     a_to_core(1)
     a_to_core(0)
     a_to_core(2)

time: 73 us -> 72.7 us (level)
  no operation moved by 1% of the time
where the time goes in v5:
time: 72.7 us; the launch traced here: 72.6 us
  Pallas kernels  71.3 us (98%)
  between operations  1.29 us (2%)
    pallas_call x1, Pallas kernels, on_device(): pl.pallas_call(kernel, out_shape=(VMEM((3, 1, 1, ATOMS), F32),) + tuple((...  69.6 us
    pallas_call x1, Pallas kernels, on_device(): pl.pallas_call(unpack, out_shape=(shape(3, 1, 1, ATOMS), shape(8, 512), s...  1.67 us

profile of v5, /device:TPU:1, one launch (start us, length us, event | category | flops | bytes accessed | tf_op | source)
XLA Modules:
  0.0 72.6 jit_solution(1034374179024443836)
XLA Ops:
  1.3 69.6 %step.1 = (f32[3,1,1,128]{3,2,1,0:T(1,128)S(1)}, f32[576,512]{1,0:T(8,128)S(1)}, f32[576,512]{1,0:T(8,128)S(1)}, f32[192,512]{1,0:T(8,128)S(1)}) custom-call(f32[3,1,1,128]{3,2,1,0:T(1,128)} %pos_in.1, s32[1,1,128]{2,1,0:T(1,128)} %spec_in.1, s32[1,1,128]{2,1,0:T(1,128)} %exp_in.1, s32[1,1,256]{2,1,0:T(1,128)} %cen_in.1, s32[1,1,256]{2,1,0:T(1,128)} %nbr_in.1, ...), custom_call_target="tpu_custom_call" | custom-call | tf_op jit(solution)/shard_map/step/pallas_call | solution.py:639
  70.9 1.7 %unpack.1 = (f32[3,1,1,128]{3,2,1,0:T(1,128)}, f32[8,512]{1,0:T(8,128)}, f32[5,512]{1,0:T(8,128)}, f32[5,512]{1,0:T(8,128)}, f32[2,64,512]{2,1,0:T(8,128)}, /*index=5*/f32[2,576,512]{2,1,0:T(8,128)}, f32[1,512]{1,0:T(1,128)}) custom-call(f32[3,1,1,128]{3,2,1,0:T(1,128)S(1)} %get-tuple-element.18.f_ref, f32[576,512]{1,0:T(8,128)S(1)} %get-tuple-element.19.g1_ref, ...), custom_call_target="tpu_custom_call" | custom-call | tf_op jit(solution)/shard_map/unpack/pallas_call | solution.py:651

commit v6 on v5

--- a/solution.py
+++ b/solution.py
@@ -534,8 +534,8 @@
 
     rest(1 - core, 0)
     start_core(2)
+    step(0, a_to_b)
     rest(core, 1)
-    step(0, a_to_b)
     core_to_a(2)
     step(1, a_to_b_whole)
     step(0, b_to_c)

time: 72.7 us -> 72.7 us (level)
  no operation moved by 1% of the time
where the time goes in v6:
time: 72.7 us; the launch traced here: 72.6 us
  Pallas kernels  71.3 us (98%)
  between operations  1.29 us (2%)
    pallas_call x1, Pallas kernels, on_device(): pl.pallas_call(kernel, out_shape=(VMEM((3, 1, 1, ATOMS), F32),) + tuple((...  69.6 us
    pallas_call x1, Pallas kernels, on_device(): pl.pallas_call(unpack, out_shape=(shape(3, 1, 1, ATOMS), shape(8, 512), s...  1.67 us

profile of v6, /device:TPU:1, one launch (start us, length us, event | category | flops | bytes accessed | tf_op | source)
XLA Modules:
  0.0 72.6 jit_solution(8701533465075033053)
XLA Ops:
  1.3 69.6 %step.1 = (f32[3,1,1,128]{3,2,1,0:T(1,128)S(1)}, f32[576,512]{1,0:T(8,128)S(1)}, f32[576,512]{1,0:T(8,128)S(1)}, f32[192,512]{1,0:T(8,128)S(1)}) custom-call(f32[3,1,1,128]{3,2,1,0:T(1,128)} %pos_in.1, s32[1,1,128]{2,1,0:T(1,128)} %spec_in.1, s32[1,1,128]{2,1,0:T(1,128)} %exp_in.1, s32[1,1,256]{2,1,0:T(1,128)} %cen_in.1, s32[1,1,256]{2,1,0:T(1,128)} %nbr_in.1, ...), custom_call_target="tpu_custom_call" | custom-call | tf_op jit(solution)/shard_map/step/pallas_call | solution.py:639
  70.9 1.7 %unpack.1 = (f32[3,1,1,128]{3,2,1,0:T(1,128)}, f32[8,512]{1,0:T(8,128)}, f32[5,512]{1,0:T(8,128)}, f32[5,512]{1,0:T(8,128)}, f32[2,64,512]{2,1,0:T(8,128)}, /*index=5*/f32[2,576,512]{2,1,0:T(8,128)}, f32[1,512]{1,0:T(1,128)}) custom-call(f32[3,1,1,128]{3,2,1,0:T(1,128)S(1)} %get-tuple-element.18.f_ref, f32[576,512]{1,0:T(8,128)S(1)} %get-tuple-element.19.g1_ref, ...), custom_call_target="tpu_custom_call" | custom-call | tf_op jit(solution)/shard_map/unpack/pallas_call | solution.py:651
